TPU v7x, 256 devices: a whole 4x4x8 slice. The times are simulated.
256 devices in a mesh: dp: 128 (over z, x, y), mp: 2 (over core).
Axes of the slice: x: 4, y: 4, z: 8, core: 2. Of those that a mesh axis runs over, the one named last changes fastest.
Arguments:
- points: bfloat16 [65536, 512], P('dp'), may hold values from -24 to 24
- patch_of: int32 [65536, 1], P('dp'), may hold values from 0 to 127; in each aligned block of 512 rows (0 to 511, 512 to 1023, ...) at most 8 rows name the same one
- qkv_weight: bfloat16 [512, 3, 512], P(None, None, 'mp'), may hold values from -10 to 10
- proj_weight: bfloat16 [512, 512], P('mp'), may hold values from -0.25 to 0.25
- fc1_weight: bfloat16 [512, 2048], P(None, 'mp'), may hold values from -0.25 to 0.25
- fc2_weight: bfloat16 [2048, 512], P('mp'), may hold values from -0.125 to 0.125
- cotangent: bfloat16 [65536, 512], P('dp'), may hold values from -24 to 24
Outputs:
- block_out: bfloat16 [65536, 512], P('dp')
- grad_qkv: float32 [512, 3, 512], P('dp', None, 'mp')
- grad_proj: float32 [512, 512], P('mp', 'dp')
- grad_fc1: float32 [512, 2048], P('dp', 'mp')
- grad_fc2: float32 [2048, 512], P('mp', 'dp')
Inputs may be any that keep to these rules, and one draw needn't show every extreme that they name: `patch_of`: in each aligned block of 512 rows (the rows of one device) no patch is named by more than 8 rows, a bound that some block reaches; every patch is named by some row, so a patch holds 1 to 1024 points.
All inputs are finite; a program needn't handle non-finite values.
Results may differ from a plain program's by a relative error of at most 0.035.
The roundings to bfloat16 on the way count: a program that leaves them out, or rounds other values in their place, can miss the bound.
Values may be sent and summed in bfloat16 or wider, within the bound.
A program may use at most 128 MiB of HBM per device.

v0:
```python
import math

import jax
import jax.numpy as jnp
from jax import lax
from jax.sharding import PartitionSpec as P

HEAD_DIM = 16
PATCH = 1024


EPS = 1e-05
GELU_C = math.sqrt(2.0 / math.pi)


def normalize(values):
    center = values - jnp.mean(values, axis=-1, keepdims=True)
    inverse = lax.rsqrt(jnp.mean(center * center, axis=-1, keepdims=True) + EPS)
    return (center * inverse, inverse)


def normalize_back(normed, inverse, upstream):
    mean_grad = jnp.mean(upstream, axis=-1, keepdims=True)
    mean_mixed = jnp.mean(upstream * normed, axis=-1, keepdims=True)
    return inverse * (upstream - mean_grad - normed * mean_mixed)


def gelu_both(values):
    cubed_input = values * values * values
    tangent = jnp.tanh(GELU_C * (values + 0.044715 * cubed_input))
    output = 0.5 * values * (1.0 + tangent)
    derivative = 0.5 * (1.0 + tangent) + 0.5 * values * (1.0 - tangent * tangent) * GELU_C * (
        1.0 + 3.0 * 0.044715 * values * values
    )
    return (output, derivative)


def grouped(tensor):
    length = tensor.shape[0]
    blocks = tensor.shape[1] // (4 * HEAD_DIM)
    return tensor.reshape(length, blocks, 4, HEAD_DIM).transpose(1, 0, 2, 3)


def ungrouped(tensor):
    blocks, length = (tensor.shape[0], tensor.shape[1])
    return tensor.transpose(1, 0, 2, 3).reshape(length, blocks * 4 * HEAD_DIM)


def head_scores(queries, keys, occupied):
    scores = jnp.einsum(
        "qhd,khd->hqk", queries, keys, preferred_element_type=jnp.float32
    ) * HEAD_DIM ** (-0.5)
    return jnp.where(occupied[None, None, :], scores, -1e30)


def attend(queries, keys, values, occupied):

    def one_group(operands):
        group_query, group_key, group_value = operands
        scores = head_scores(group_query, group_key, occupied)
        maxima = jnp.max(scores, axis=2, keepdims=True)
        exponent = jnp.exp(scores - maxima)
        totals = jnp.sum(exponent, axis=2, keepdims=True)
        weights = (exponent / totals).astype(jnp.bfloat16)
        result = jnp.einsum(
            "hqk,khd->qhd", weights, group_value, preferred_element_type=jnp.float32
        )
        return (result.astype(jnp.bfloat16), maxima, totals)

    outputs, maxima, totals = lax.map(one_group, (grouped(queries), grouped(keys), grouped(values)))
    return (ungrouped(outputs), maxima, totals)


def attend_back(queries, keys, values, occupied, attended, d_attended, maxima, totals):

    def one_group(operands):
        group_query, group_key, group_value, group_out, group_grad, group_max, group_total = (
            operands
        )
        scores = head_scores(group_query, group_key, occupied)
        weights = jnp.exp(scores - group_max) / group_total
        rounded = weights.astype(jnp.bfloat16)
        d_weights = jnp.einsum(
            "qhd,khd->hqk", group_grad, group_value, preferred_element_type=jnp.float32
        )
        delta = jnp.einsum("qhd,qhd->hq", group_grad, group_out, preferred_element_type=jnp.float32)
        d_scores = (weights * (d_weights - delta[:, :, None]) * HEAD_DIM ** (-0.5)).astype(
            jnp.bfloat16
        )
        grad_query = jnp.einsum(
            "hqk,khd->qhd", d_scores, group_key, preferred_element_type=jnp.float32
        ).astype(jnp.bfloat16)
        grad_key = jnp.einsum(
            "hqk,qhd->khd", d_scores, group_query, preferred_element_type=jnp.float32
        ).astype(jnp.bfloat16)
        grad_value = jnp.einsum(
            "hqk,qhd->khd", rounded, group_grad, preferred_element_type=jnp.float32
        ).astype(jnp.bfloat16)
        return (grad_query, grad_key, grad_value)

    results = lax.map(
        one_group,
        (
            grouped(queries),
            grouped(keys),
            grouped(values),
            grouped(attended),
            grouped(d_attended),
            maxima,
            totals,
        ),
    )
    return (ungrouped(results[0]), ungrouped(results[1]), ungrouped(results[2]))


def contract_rows(left, right):
    return lax.dot_general(
        left, right, (((0,), (0,)), ((), ())), preferred_element_type=jnp.float32
    )


def contract_cols(left, right):
    return lax.dot_general(
        left, right, (((1,), (1,)), ((), ())), preferred_element_type=jnp.float32
    )


def per_device(points, patch_of, qkv_weight, proj_weight, fc1_weight, fc2_weight, cotangent):
    sources = lax.axis_size("dp")
    features = points.shape[1]
    bucket = PATCH // sources
    target = patch_of[:, 0]
    member = (target[:, None] == jnp.arange(sources, dtype=jnp.int32)[None, :]).astype(jnp.int32)
    earlier = jnp.cumsum(member, axis=0) - member
    within = jnp.sum(earlier * member, axis=1)
    slot_index = target * bucket + within
    empty_rows = jnp.zeros((PATCH, features), jnp.bfloat16)
    send_points = empty_rows.at[slot_index].set(points).reshape(sources, bucket, features)
    send_upstream = empty_rows.at[slot_index].set(cotangent).reshape(sources, bucket, features)
    send_flags = jnp.zeros((PATCH,), jnp.bfloat16).at[slot_index].set(1.0).reshape(sources, bucket)
    got_points, got_upstream, got_flags = (
        lax.all_to_all(send_points, "dp", split_axis=0, concat_axis=0, tiled=True),
        lax.all_to_all(send_upstream, "dp", split_axis=0, concat_axis=0, tiled=True),
        lax.all_to_all(send_flags, "dp", split_axis=0, concat_axis=0, tiled=True),
    )
    rows_in = got_points.reshape(PATCH, features)
    upstream = got_upstream.reshape(PATCH, features)
    occupied = got_flags.reshape(PATCH) > 0
    wide_in = rows_in.astype(jnp.float32)
    normed_one, inverse_one = normalize(wide_in)
    normed_in = normed_one.astype(jnp.bfloat16)
    projected = jnp.einsum(
        "rd,dje->jre", normed_in, qkv_weight, preferred_element_type=jnp.float32
    ).astype(jnp.bfloat16)
    attended, maxima, totals = attend(projected[0], projected[1], projected[2], occupied)
    partial_attn = jnp.dot(attended, proj_weight, preferred_element_type=jnp.float32)
    mixed = wide_in + lax.psum(partial_attn, "mp")
    normed_two, inverse_two = normalize(mixed)
    normed_mid = normed_two.astype(jnp.bfloat16)
    pre_act = jnp.dot(normed_mid, fc1_weight, preferred_element_type=jnp.float32)
    activation, derivative = gelu_both(pre_act)
    act_low = activation.astype(jnp.bfloat16)
    partial_mlp = jnp.dot(act_low, fc2_weight, preferred_element_type=jnp.float32)
    block_rows = (
        mixed + lax.psum(partial_mlp.astype(jnp.bfloat16), "mp").astype(jnp.float32)
    ).astype(jnp.bfloat16)
    returned = lax.all_to_all(
        block_rows.reshape(sources, bucket, features), "dp", split_axis=0, concat_axis=0, tiled=True
    )
    block_out = returned.reshape(PATCH, features)[slot_index]
    grad_fc2 = contract_rows(act_low, upstream)
    d_pre = (contract_cols(upstream, fc2_weight) * derivative).astype(jnp.bfloat16)
    grad_fc1 = contract_rows(normed_mid, d_pre)
    partial_norm = contract_cols(d_pre, fc1_weight)
    back_norm = lax.psum(partial_norm.astype(jnp.bfloat16), "mp").astype(jnp.float32)
    d_mixed = (
        upstream.astype(jnp.float32) + normalize_back(normed_two, inverse_two, back_norm)
    ).astype(jnp.bfloat16)
    grad_proj = contract_rows(attended, d_mixed)
    d_attended = contract_cols(d_mixed, proj_weight).astype(jnp.bfloat16)
    grad_query, grad_key, grad_value = attend_back(
        projected[0], projected[1], projected[2], occupied, attended, d_attended, maxima, totals
    )
    stacked = jnp.stack([grad_query, grad_key, grad_value])
    grad_qkv = jnp.einsum("rd,jre->dje", normed_in, stacked, preferred_element_type=jnp.float32)
    grad_qkv, grad_proj, grad_fc1, grad_fc2 = (
        lax.psum_scatter(grad_qkv, "dp", scatter_dimension=0, tiled=True),
        lax.psum_scatter(grad_proj, "dp", scatter_dimension=1, tiled=True),
        lax.psum_scatter(grad_fc1, "dp", scatter_dimension=0, tiled=True),
        lax.psum_scatter(grad_fc2, "dp", scatter_dimension=1, tiled=True),
    )
    return (block_out, grad_qkv, grad_proj, grad_fc1, grad_fc2)


def solution(mesh):
    placed = (
        P("dp", None),
        P("dp", None),
        P(None, None, "mp"),
        P("mp", None),
        P(None, "mp"),
        P("mp", None),
        P("dp", None),
    )
    return jax.shard_map(
        per_device,
        mesh=mesh,
        in_specs=placed,
        out_specs=(P("dp", None), P("dp", None, "mp"), P("mp", "dp"), P("dp", "mp"), P("mp", "dp")),
        check_vma=False,
    )
```

profile of v0, /device:TPU:1, one launch (start us, length us, event | category | flops | bytes accessed | tf_op | source)
XLA Modules:
  0.0 599.4 jit_solution(16739811775551647199)
XLA Ops:
  14.6 16.3 %all-to-all-start.1 = ((bf16[128,1,8]{2,1,0:T(2,128)(2,1)}), bf16[128,1,8]{2,1,0:T(2,128)(2,1)S(1)}, u32[]{:S(2)}, u32[]{:S(2)}) async-start(bf16[128,1,8]{2,1,0:T(2,128)(2,1)} %all_to_all.20), calls=%async_computation.1 | async-start | bytes 131072 | tf_op jit(solution)/shard_map/all_to_all | solution.py:144
  34.9 6.7 %all-to-all-done.1 = bf16[128,1,8]{2,1,0:T(2,128)(2,1)S(1)} async-done(((bf16[128,1,8]{2,1,0:T(2,128)(2,1)}), bf16[128,1,8]{2,1,0:T(2,128)(2,1)S(1)}, u32[]{:S(2)}, u32[]{:S(2)}) %all-to-all-start.1) | async-done | bytes 2080 | tf_op jit(solution)/shard_map/all_to_all | solution.py:144
  41.6 6.5 %all-to-all-start = ((bf16[128,8,512]{2,1,0:T(8,128)(2,1)}), bf16[128,8,512]{2,1,0:T(8,128)(2,1)S(1)}, u32[]{:S(2)}, u32[]{:S(2)}) async-start(bf16[128,8,512]{2,1,0:T(8,128)(2,1)} %bitcast.31), calls=%async_computation | async-start | bytes 2097152 | tf_op jit(solution)/shard_map/all_to_all | solution.py:142
  48.7 27.1 %all-to-all-done = bf16[128,8,512]{2,1,0:T(8,128)(2,1)S(1)} async-done(((bf16[128,8,512]{2,1,0:T(8,128)(2,1)}), bf16[128,8,512]{2,1,0:T(8,128)(2,1)S(1)}, u32[]{:S(2)}, u32[]{:S(2)}) %all-to-all-start) | async-done | bytes 1048608 | tf_op jit(solution)/shard_map/all_to_all | solution.py:142
  79.6 48.3 %while.28 = (s32[]{:T(128)}, bf16[4,1024,4,16]{1,3,2,0:T(8,128)(2,1)S(1)}, f32[4,4,1024,1]{2,1,3,0:T(4,128)S(1)}, f32[4,4,1024,1]{2,1,3,0:T(4,128)S(1)}, bf16[4,...) while((s32[]{:T(128)}, ...), condition=%wide.region_10.11_spmd, body=%wide.region_7.10_spmd.sunk | while | flops 318824448 | bytes 51008616 | solution.py:70
  86.9 4.8 fusion.144
  99.0 4.8 fusion.144
  111.1 4.8 fusion.144
  133.8 9.2 %all-to-all-start.3 = ((bf16[128,8,512]{2,1,0:T(8,128)(2,1)}), bf16[128,8,512]{2,1,0:T(8,128)(2,1)}, u32[]{:S(2)}, u32[]{:S(2)}) async-start(bf16[128,8,512]{2,1,0:T(8,128)(2,1)} %bitcast.209), calls=%async_computation.3 | async-start | bytes 2097152 | tf_op jit(solution)/shard_map/all_to_all | solution.py:143
  143.1 16.8 %all-reduce.10.cloned.1.call-done = f32[1024,512]{1,0:T(8,128)} async-done(((f32[1024,512]{1,0:T(8,128)}), f32[1024,512]{1,0:T(8,128)}) %all-reduce.10.cloned.1.call-update) | async-done | bytes 2097168 | tf_op jit(solution)/shard_map/psum | solution.py:157
  169.0 5.4 fusion.60
  186.9 23.9 %all-reduce.14.cloned.1.call-done = (bf16[1024,512]{1,0:T(8,128)(2,1)}, bf16[1024,512]{1,0:T(8,128)(2,1)}) async-done(((bf16[1024,512]{1,0:T(8,128)(2,1)}, bf16[1024,512]{1,0:T(8,128)(2,1)}), (bf16[1024,512]{1,0:T(8,128)(2,1)}, bf16[1024,512]{1,0:T(8,128)(2,1)})) %all-reduce.14.cloned.1.call-update) | async-done | bytes 2097168 | tf_op jit(solution)/shard_map/psum | solution.py:165
  220.1 96.2 %while.29 = (s32[]{:T(128)}, bf16[4,1024,4,16]{1,3,2,0:T(8,128)(2,1)}, bf16[4,1024,4,16]{1,3,2,0:T(8,128)(2,1)}, bf16[4,1024,4,16]{1,3,2,0:T(8,128)(2,1)S(1)}, b...) while((s32[]{:T(128)}, ...), condition=%wide.region_20.21_spmd, body=%wide.region_19.20_spmd.sunk | while | flops 709292032 | bytes 144316592 | solution.py:101
  225.2 5.7 copy-done.2
  232.1 7.3 %multiply_convert_fusion.5 = bf16[4,1024,1024]{2,1,0:T(8,128)(2,1)S(1)} fusion(f32[4,1024,1024]{2,1,0:T(8,128)} %copy-done.2, f32[4,1024]{1,0:T(4,128)S(1)} %fusion.155, bf16[4,1024,4,16]{1,3,2,0:T(8,128)(2,1)} %get-tuple-element.379, s32[]{:T(128)S(6)} %copy.74, bf16[4,1024,4,16]{1,3,2,0:T(8,128)(2,1)S(1)} %get-tuple-element.378), kind=kOutput, calls=%fused_computation.26.clone.1 | convolution fusion | flops 150994944 | bytes 25445376 | tf_op jit(solution)/shard_map/while/body/eval_jaxpr/qhd,khd->hqk/dot_general | solution.py:83
  249.1 5.7 copy-done.2
  256.1 7.3 %multiply_convert_fusion.5 = bf16[4,1024,1024]{2,1,0:T(8,128)(2,1)S(1)} fusion(f32[4,1024,1024]{2,1,0:T(8,128)} %copy-done.2, f32[4,1024]{1,0:T(4,128)S(1)} %fusion.155, bf16[4,1024,4,16]{1,3,2,0:T(8,128)(2,1)} %get-tuple-element.379, s32[]{:T(128)S(6)} %copy.74, bf16[4,1024,4,16]{1,3,2,0:T(8,128)(2,1)S(1)} %get-tuple-element.378), kind=kOutput, calls=%fused_computation.26.clone.1 | convolution fusion | flops 150994944 | bytes 25445376 | tf_op jit(solution)/shard_map/while/body/eval_jaxpr/qhd,khd->hqk/dot_general | solution.py:83
  273.1 5.7 copy-done.2
  280.0 7.3 %multiply_convert_fusion.5 = bf16[4,1024,1024]{2,1,0:T(8,128)(2,1)S(1)} fusion(f32[4,1024,1024]{2,1,0:T(8,128)} %copy-done.2, f32[4,1024]{1,0:T(4,128)S(1)} %fusion.155, bf16[4,1024,4,16]{1,3,2,0:T(8,128)(2,1)} %get-tuple-element.379, s32[]{:T(128)S(6)} %copy.74, bf16[4,1024,4,16]{1,3,2,0:T(8,128)(2,1)S(1)} %get-tuple-element.378), kind=kOutput, calls=%fused_computation.26.clone.1 | convolution fusion | flops 150994944 | bytes 25445376 | tf_op jit(solution)/shard_map/while/body/eval_jaxpr/qhd,khd->hqk/dot_general | solution.py:83
  297.1 5.7 copy-done.2
  304.0 7.3 %multiply_convert_fusion.5 = bf16[4,1024,1024]{2,1,0:T(8,128)(2,1)S(1)} fusion(f32[4,1024,1024]{2,1,0:T(8,128)} %copy-done.2, f32[4,1024]{1,0:T(4,128)S(1)} %fusion.155, bf16[4,1024,4,16]{1,3,2,0:T(8,128)(2,1)} %get-tuple-element.379, s32[]{:T(128)S(6)} %copy.74, bf16[4,1024,4,16]{1,3,2,0:T(8,128)(2,1)S(1)} %get-tuple-element.378), kind=kOutput, calls=%fused_computation.26.clone.1 | convolution fusion | flops 150994944 | bytes 25445376 | tf_op jit(solution)/shard_map/while/body/eval_jaxpr/qhd,khd->hqk/dot_general | solution.py:83
  321.5 13.7 %all-to-all-start.2 = ((bf16[128,8,512]{2,1,0:T(8,128)(2,1)}), bf16[128,8,512]{2,1,0:T(8,128)(2,1)S(1)}, u32[]{:S(2)}, u32[]{:S(2)}) async-start(bf16[128,8,512]{2,1,0:T(8,128)(2,1)} %get-tuple-element.176), calls=%async_computation.2 | async-start | bytes 2097152 | tf_op jit(solution)/shard_map/all_to_all | solution.py:167
  336.5 39.8 %all-to-all-done.2 = bf16[128,8,512]{2,1,0:T(8,128)(2,1)S(1)} async-done(((bf16[128,8,512]{2,1,0:T(8,128)(2,1)}), bf16[128,8,512]{2,1,0:T(8,128)(2,1)S(1)}, u32[]{:S(2)}, u32[]{:S(2)}) %all-to-all-start.2) | async-done | bytes 1048608 | tf_op jit(solution)/shard_map/all_to_all | solution.py:167
  378.9 208.4 %all-reduce.12.cloned.1.call-done = (f32[512,3,256]{2,0,1:T(8,128)}, f32[256,512]{0,1:T(8,128)}, f32[512,1024]{1,0:T(8,128)}, f32[1024,512]{0,1:T(8,128)}) async-done(((f32[512,3,256]{2,0,1:T(8,128)}, f32[256,512]{0,1:T(8,128)}, f32[512,1024]{1,0:T(8,128)}, f32[1024,512]{0,1:T(8,128)}), (f32[512,3,256]{2,0,1:T(8,128)}, f32[256,512]{0,1:T(8,128)}, f32[512,1024]{1,0:T(8,128)}, ...) | async-done | bytes 6291472
  (153 shorter events, 143.7 us)
Async XLA Ops:
  7.2 158.6 %copy-start = (bf16[1024,512]{1,0:T(8,128)(2,1)S(1)}, bf16[1024,512]{1,0:T(8,128)(2,1)}, u32[]{:S(2)}) copy-start(bf16[1024,512]{1,0:T(8,128)(2,1)} %param.16) | copy-start | bytes 3145732
  8.3 69.0 %copy-start.20 = (bf16[512,3,256]{2,0,1:T(8,128)(2,1)S(1)}, bf16[512,3,256]{2,0,1:T(8,128)(2,1)}, u32[]{:S(2)}) copy-start(bf16[512,3,256]{2,0,1:T(8,128)(2,1)} %param.13) | copy-start | bytes 2359300
  10.1 66.7 %copy-start.12 = (s32[512,1]{0,1:T(1,128)}, s32[512,1]{0,1:T(1,128)S(1)}, u32[]{:S(2)}) copy-start(s32[512,1]{0,1:T(1,128)S(1)} %compare_select_fusion) | copy-start | bytes 6148
  14.6 27.0 %all-to-all-start.1 = ((bf16[128,1,8]{2,1,0:T(2,128)(2,1)}), bf16[128,1,8]{2,1,0:T(2,128)(2,1)S(1)}, u32[]{:S(2)}, u32[]{:S(2)}) async-start(bf16[128,1,8]{2,1,0:T(2,128)(2,1)} %all_to_all.20), calls=%async_computation.1 | async-start | bytes 131072 | tf_op jit(solution)/shard_map/all_to_all | solution.py:144
  41.6 34.1 %all-to-all-start = ((bf16[128,8,512]{2,1,0:T(8,128)(2,1)}), bf16[128,8,512]{2,1,0:T(8,128)(2,1)S(1)}, u32[]{:S(2)}, u32[]{:S(2)}) async-start(bf16[128,8,512]{2,1,0:T(8,128)(2,1)} %bitcast.31), calls=%async_computation | async-start | bytes 2097152 | tf_op jit(solution)/shard_map/all_to_all | solution.py:142
  48.1 111.8 %all-reduce.10.cloned.1.call-start = ((), (), s32[]{:S(2)}) async-start(), calls=%async_computation.4 | async-start | bytes 4194304 | tf_op jit(solution)/shard_map/psum | solution.py:157
  79.6 48.4 %copy-start.11 = (bf16[256,512]{1,0:T(8,128)(2,1)S(1)}, bf16[256,512]{1,0:T(8,128)(2,1)}, u32[]{:S(2)}) copy-start(bf16[256,512]{1,0:T(8,128)(2,1)} %param.14) | copy-start | bytes 786436
  128.0 15.1 %copy-start.5 = (bf16[4,1024,4,16]{1,3,2,0:T(8,128)(2,1)}, bf16[4,1024,4,16]{1,3,2,0:T(8,128)(2,1)S(1)}, u32[]{:S(2)}) copy-start(bf16[4,1024,4,16]{1,3,2,0:T(8,128)(2,1)S(1)} %get-tuple-element.354) | copy-start | bytes 1572868
  128.0 15.1 %copy-start.7 = (bf16[4,1024,4,16]{1,3,2,0:T(8,128)(2,1)}, bf16[4,1024,4,16]{1,3,2,0:T(8,128)(2,1)S(1)}, u32[]{:S(2)}) copy-start(bf16[4,1024,4,16]{1,3,2,0:T(8,128)(2,1)S(1)} %get-tuple-element.399) | copy-start | bytes 1572868
  128.0 15.1 %copy-start.9 = (bf16[4,1024,4,16]{1,3,2,0:T(8,128)(2,1)}, bf16[4,1024,4,16]{1,3,2,0:T(8,128)(2,1)S(1)}, u32[]{:S(2)}) copy-start(bf16[4,1024,4,16]{1,3,2,0:T(8,128)(2,1)S(1)} %get-tuple-element.400) | copy-start | bytes 1572868
  133.8 35.2 %all-to-all-start.3 = ((bf16[128,8,512]{2,1,0:T(8,128)(2,1)}), bf16[128,8,512]{2,1,0:T(8,128)(2,1)}, u32[]{:S(2)}, u32[]{:S(2)}) async-start(bf16[128,8,512]{2,1,0:T(8,128)(2,1)} %bitcast.209), calls=%async_computation.3 | async-start | bytes 2097152 | tf_op jit(solution)/shard_map/all_to_all | solution.py:143
  143.0 67.8 %all-reduce.14.cloned.1.call-start = ((), (), s32[]{:S(2)}) async-start(), calls=%async_computation.6 | async-start | bytes 4194304 | tf_op jit(solution)/shard_map/psum | solution.py:165
  169.0 6.7 %copy-start.19 = (bf16[512,1024]{1,0:T(8,128)(2,1)S(1)}, bf16[512,1024]{1,0:T(8,128)(2,1)}, u32[]{:S(2)}) copy-start(bf16[512,1024]{1,0:T(8,128)(2,1)} %param.15) | copy-start | bytes 3145732
  178.0 409.3 %all-reduce.12.cloned.1.call-start = ((), (), s32[]{:S(2)}) async-start(), calls=%async_computation.5 | async-start | bytes 12582912
  220.1 98.9 %copy-start.4 = (bf16[128,8,512]{2,1,0:T(8,128)(2,1)S(1)}, bf16[128,8,512]{2,1,0:T(8,128)(2,1)}, u32[]{:S(2)}) copy-start(bf16[128,8,512]{2,1,0:T(8,128)(2,1)} %copy-done.3) | copy-start | bytes 3145732
  220.1 98.9 %copy-start.15 = (f32[1024]{0:T(1024)S(1)}, f32[1024]{0:T(1024)}, u32[]{:S(2)}) copy-start(f32[1024]{0:T(1024)} %copy-done.14) | copy-start | bytes 12292
  220.1 98.9 %copy-start.17 = (f32[1024]{0:T(1024)S(1)}, f32[1024]{0:T(1024)}, u32[]{:S(2)}) copy-start(f32[1024]{0:T(1024)} %copy-done.16) | copy-start | bytes 12292
  225.2 5.7 copy-start.2
  249.1 5.7 copy-start.2
  273.1 5.7 copy-start.2
  321.4 13.8 %copy-start.21 = (u32[256]{0:T(256)S(1)}, u32[256]{0:T(256)}, u32[]{:S(2)}) copy-start(u32[256]{0:T(256)} %constant.85) | copy-start | bytes 3076
  321.4 15.0 %copy-start.13 = (s32[512,1]{0,1:T(1,128)S(1)}, s32[512,1]{0,1:T(1,128)}, u32[]{:S(2)}) copy-start(s32[512,1]{0,1:T(1,128)} %copy-done.12) | copy-start | bytes 6148
  321.5 271.2 %copy-start.1 = (bf16[1024,512]{1,0:T(8,128)(2,1)S(1)}, bf16[1024,512]{1,0:T(8,128)(2,1)}, u32[]{:S(2)}) copy-start(bf16[1024,512]{1,0:T(8,128)(2,1)} %param.16) | copy-start | bytes 3145732
  321.5 54.8 %all-to-all-start.2 = ((bf16[128,8,512]{2,1,0:T(8,128)(2,1)}), bf16[128,8,512]{2,1,0:T(8,128)(2,1)S(1)}, u32[]{:S(2)}, u32[]{:S(2)}) async-start(bf16[128,8,512]{2,1,0:T(8,128)(2,1)} %get-tuple-element.176), calls=%async_computation.2 | async-start | bytes 2097152 | tf_op jit(solution)/shard_map/all_to_all | solution.py:167
  (11 other events, 34.7 us)
Sparse Core Ops, SparseCore 0:
  130.0 29.8 all-reduce.9
  178.1 32.6 all-reduce.13
  321.6 265.6 all-reduce.11
where the time goes:
time: 608 us; the launch traced here: 599 us
  waiting for transfers between devices  323 us (53%)
  matrix products  129 us (21%)
  local copies, waits for them, and re-layouts  54.5 us (9%)
  starting transfers between devices  46 us (8%)
  other arithmetic  31.2 us (5%)
  between operations  15.1 us (2%)
    unnamed x4, waiting for transfers between devices  208 us
    all_to_all x1, waiting for transfers between devices, per_device(): lax.all_to_all(block_rows.reshape(sources, bucket, features), 'dp', split...  39.8 us
    dot_general x4, matrix products, one_group(): jnp.einsum('qhd,khd->hqk', group_grad, group_value, preferred_element_typ...  29.1 us
    dot_general x8, matrix products, head_scores(): jnp.einsum('qhd,khd->hqk', queries, keys, preferred_element_type=jnp.floa...  28.6 us
    all_to_all x1, waiting for transfers between devices, per_device(): lax.all_to_all(send_points, 'dp', split_axis=0, concat_axis=0, tiled=True)  27.1 us
    psum x1, waiting for transfers between devices, per_device(): lax.psum(partial_mlp.astype(jnp.bfloat16), 'mp').astype(jnp.float32)  23.9 us
    while x8, local copies, waits for them, and re-layouts  22.9 us
    dot_general x4, matrix products, one_group(): jnp.einsum('hqk,khd->qhd', weights, group_value, preferred_element_type=j...  19.3 us
  transfers between devices with their start and end apart: 7, of which 7 were waited for; matrix products, arithmetic and copies ran while one was open for 4% of the time, Pallas kernels for 0%

commit v1 on v0

v1 whole, which is shorter than its diff:
```python
import functools
import math

import jax
import jax.numpy as jnp
from jax import lax
from jax.experimental import pallas as pl
from jax.experimental.pallas import tpu as pltpu
from jax.sharding import PartitionSpec as P

MESH = pl.DeviceIdType.MESH
F32 = jnp.float32
BF16 = jnp.bfloat16
VMEM = pl.BlockSpec(memory_space=pltpu.VMEM)

HEADS = 16
HEAD_DIM = 16
PATCH = 1024
ROWS = 512
D = 512
FF = 1024
EPS = 1e-05
GELU_C = math.sqrt(2.0 / math.pi)
EXP2_SCALE = HEAD_DIM**-0.5 * math.log2(math.e)
EMPTY = 64.0
MASKED = -1e30
NX, NY, NZ = 4, 4, 8
PAIRS = 64
GW = 2304
QW = 768


def dot(left, right, dims):
    return lax.dot_general(left, right, (dims, ((), ())), preferred_element_type=F32)


NN = ((1,), (0,))
NT = ((1,), (1,))
TN = ((0,), (0,))


def params(**more):
    return pltpu.CompilerParams(vmem_limit_bytes=56 << 20, **more)


def normalize(values):
    center = values - jnp.mean(values, axis=-1, keepdims=True)
    inverse = lax.rsqrt(jnp.mean(center * center, axis=-1, keepdims=True) + EPS)
    return center * inverse, inverse


def split3(x):
    a = x.astype(BF16)
    r = x - a.astype(F32)
    b = r.astype(BF16)
    return a, b, (r - b.astype(F32)).astype(BF16)


def pack(rows):
    n = rows.shape[0] // 8
    pieces = rows.reshape(n, 8, D)
    return jnp.concatenate([pieces[:, :, : D // 2], pieces[:, :, D // 2 :]], axis=1).astype(BF16)


def unpack(pieces):
    wide = pieces.astype(F32)
    n = wide.shape[0]
    return jnp.concatenate([wide[:, :8], wide[:, 8:]], axis=2).reshape(8 * n, D)


def pair_barrier(me, core, extra=()):
    barrier = pltpu.get_barrier_semaphore()
    parity = lax.rem(core + me, 2)

    def greet(i, carry):
        other = 2 * lax.rem(lax.div(me, 2) + i, PAIRS) + parity
        pl.semaphore_signal(barrier, inc=1, device_id=(other, core), device_id_type=MESH)
        return carry

    lax.fori_loop(1, PAIRS, greet, 0)

    @pl.when(core == 1)
    def _():
        other = 2 * lax.div(me, 2) + parity
        pl.semaphore_signal(barrier, inc=1, device_id=(other, core), device_id_type=MESH)

    pl.semaphore_signal(barrier, inc=1, device_id=(me, 1 - core), device_id_type=MESH)
    for other in extra:
        pl.semaphore_signal(barrier, inc=1, device_id=(other, core), device_id_type=MESH)
    pl.semaphore_wait(barrier, PAIRS + core + len(extra))


def pair_sends(me, core, out, landing, send_sem, recv_sem):
    parity = lax.rem(core + me, 2)
    mine = lax.div(me, 2)

    def push(place):
        pltpu.make_async_remote_copy(
            src_ref=out.at[place],
            dst_ref=landing.at[core, mine],
            send_sem=send_sem,
            recv_sem=recv_sem,
            device_id=(2 * place + parity, core),
            device_id_type=MESH,
        ).start()

    @pl.when(core == 0)
    def _():
        pltpu.make_async_copy(out.at[mine], landing.at[core, mine], recv_sem).start()

    @pl.when(core == 1)
    def _():
        push(mine)

    def step(i, carry):
        push(lax.rem(mine + i, PAIRS))
        return carry

    lax.fori_loop(1, PAIRS, step, 0)


def pair_arrived(core, landing, recv_sem):
    pltpu.make_async_copy(landing.at[core], landing.at[core], recv_sem).wait()


def pair_sent(core, out, send_sem):
    most = out.at[pl.ds(0, PAIRS - 1)]
    pltpu.make_async_copy(most, most, send_sem).wait()

    @pl.when(core == 1)
    def _():
        pltpu.make_async_copy(out.at[0], out.at[0], send_sem).wait()


def to_sibling(me, core, landing, send_sem, recv_sem):
    return pltpu.make_async_remote_copy(
        src_ref=landing.at[core],
        dst_ref=landing.at[core],
        send_sem=send_sem,
        recv_sem=recv_sem,
        device_id=(me, 1 - core),
        device_id_type=MESH,
    )


def sibling_arrived(core, landing, recv_sem):
    pltpu.make_async_copy(landing.at[1 - core], landing.at[1 - core], recv_sem).wait()


def slot_rows(patch, me):
    member = (lax.broadcasted_iota(jnp.int32, (128, ROWS), 0) == patch).astype(BF16)
    before = (
        lax.broadcasted_iota(jnp.int32, (ROWS, ROWS), 0)
        < lax.broadcasted_iota(jnp.int32, (ROWS, ROWS), 1)
    ).astype(BF16)
    earlier = dot(member, before, NN)
    within = jnp.sum(earlier * member.astype(F32), axis=0, keepdims=True).astype(jnp.int32)
    return ((patch + me) & 1) * (PATCH // 2) + (patch >> 1) * 8 + within


def dispatch_kernel(
    points, cotangent, patch, rows_out, upstream_out, bias_out, slot_out,
    out_p, out_c, land_p, land_c, send_sem, recv_sem,
):
    me, core = lax.axis_index("dp"), lax.axis_index("mp")
    slot = slot_rows(patch[...], me)
    slot_out[...] = jnp.broadcast_to(slot, (8, ROWS))
    place = lax.broadcasted_iota(jnp.int32, (PATCH // 2, ROWS), 0) + core * (PATCH // 2)
    chosen = (place == slot).astype(BF16)
    filled = dot(chosen, jnp.ones((ROWS, 128), BF16), NN)
    fill = EMPTY * (1.0 - jnp.concatenate([filled] * (D // 128), axis=1))
    out_p[...] = pack(dot(chosen, points[...], NN) + fill)
    pair_barrier(me, core)
    pair_sends(me, core, out_p, land_p, send_sem.at[0], recv_sem.at[0])
    out_c[...] = pack(dot(chosen, cotangent[...], NN))
    pair_sends(me, core, out_c, land_c, send_sem.at[1], recv_sem.at[1])
    pair_arrived(core, land_p, recv_sem.at[0])
    first = to_sibling(me, core, land_p, send_sem.at[2], recv_sem.at[2])
    first.start()
    pair_arrived(core, land_c, recv_sem.at[1])
    second = to_sibling(me, core, land_c, send_sem.at[3], recv_sem.at[3])
    second.start()
    sibling_arrived(core, land_p, recv_sem.at[2])
    ones = jnp.ones((16, 128), BF16)
    for half in range(2):
        for part in range(2):
            pieces = slice(part * 32, part * 32 + 32)
            at = half * 512 + part * 256
            wide = unpack(land_p[half, pieces])
            empty = wide > 0.5 * EMPTY
            rows_out[at : at + 256, :] = jnp.where(empty, 0.0, wide).astype(BF16)
            count = dot(ones, jnp.where(empty[:, :128], 1.0, 0.0).astype(BF16), NT)
            first_row = lax.broadcasted_iota(jnp.int32, (16, 256), 0) == 0
            bias_out[:, at : at + 256] = jnp.where(
                first_row & (count > 0.5), MASKED, 0.0
            ).astype(BF16)
    sibling_arrived(core, land_c, recv_sem.at[3])
    for half in range(2):
        for part in range(2):
            pieces = slice(part * 32, part * 32 + 32)
            at = half * 512 + part * 256
            upstream_out[at : at + 256, :] = unpack(land_c[half, pieces]).astype(BF16)
    first.wait_send()
    second.wait_send()
    pair_sent(core, out_p, send_sem.at[0])
    pair_sent(core, out_c, send_sem.at[1])


def dispatch(points, cotangent, patch):
    pieces = pltpu.VMEM((PAIRS, 16, D // 2), BF16)
    landing = pltpu.VMEM((2, PAIRS, 16, D // 2), BF16)
    return pl.pallas_call(
        dispatch_kernel,
        out_shape=(
            jax.ShapeDtypeStruct((PATCH, D), BF16),
            jax.ShapeDtypeStruct((PATCH, D), BF16),
            jax.ShapeDtypeStruct((16, PATCH), BF16),
            jax.ShapeDtypeStruct((8, ROWS), jnp.int32),
        ),
        in_specs=[VMEM] * 3,
        out_specs=(VMEM,) * 4,
        scratch_shapes=[
            pieces,
            pieces,
            landing,
            landing,
            pltpu.SemaphoreType.DMA((4,)),
            pltpu.SemaphoreType.DMA((4,)),
        ],
        compiler_params=params(collective_id=1, has_side_effects=True),
        name="dispatch",
    )(points, cotangent, patch)


def forward_head(query, key, value, bias):
    scaled = split3(query.astype(F32) * EXP2_SCALE)
    wide_query = jnp.concatenate([*scaled, jnp.ones((16, PATCH), BF16)], axis=0)
    wide_key = jnp.concatenate([key, key, key, bias], axis=0)
    scores = dot(wide_key, wide_query, TN)
    maxima = jnp.max(scores, axis=0, keepdims=True)
    weights = jnp.exp2(scores - maxima)
    totals = jnp.sum(weights, axis=0, keepdims=True)
    result = dot(value, weights.astype(BF16), NN) / totals
    return result.astype(BF16), maxima + jnp.log2(totals)


def attend_kernel(rows, weight, bias, normed_out, qkv_out, attended_out, lse_out):
    for part in range(4):
        at = slice(part * 256, part * 256 + 256)
        normed, _ = normalize(rows[at, :].astype(F32))
        normed_out[at, :] = normed.astype(BF16)
    for j in range(3):
        projected = dot(weight[j * 256 : j * 256 + 256, :], normed_out[...], NT)
        qkv_out[j] = projected.astype(BF16).reshape(HEADS, HEAD_DIM, PATCH)
    mask = bias[...]

    def pair(i, carry):
        for u in range(2):
            h = 2 * i + u
            result, lse = forward_head(qkv_out[0, h], qkv_out[1, h], qkv_out[2, h], mask)
            attended_out[h] = result
            lse_out[h] = jnp.broadcast_to(lse, (8, PATCH))
        return carry

    lax.fori_loop(0, HEADS // 2, pair, 0)


def attend(rows, weight, bias):
    heads = (HEADS, HEAD_DIM, PATCH)
    return pl.pallas_call(
        attend_kernel,
        out_shape=(
            jax.ShapeDtypeStruct((PATCH, D), BF16),
            jax.ShapeDtypeStruct((3, *heads), BF16),
            jax.ShapeDtypeStruct(heads, BF16),
            jax.ShapeDtypeStruct((HEADS, 8, PATCH), F32),
        ),
        in_specs=[VMEM] * 3,
        out_specs=(VMEM,) * 4,
        compiler_params=params(),
        name="attend",
    )(rows, weight, bias)


def backward_head(query, key, value, bias, attended, upstream, lse):
    shape = (16, PATCH)
    row = lax.broadcasted_iota(jnp.int32, shape, 0)
    one = jnp.ones(shape, BF16)
    zero = jnp.zeros(shape, BF16)

    def stacked(*given):
        total = zero
        for at, value_at in enumerate(given):
            total = jnp.where(row == at, value_at, total)
        return total

    lse_pieces = split3(-jnp.broadcast_to(lse, shape))
    scaled = split3(query.astype(F32) * EXP2_SCALE)
    wide_query = jnp.concatenate([*scaled, stacked(one, *lse_pieces)], axis=0)
    wide_key = jnp.concatenate([key, key, key, stacked(bias, one, one, one)], axis=0)
    scale = HEAD_DIM**-0.5
    upstream_wide = upstream.astype(F32)
    delta = -scale * jnp.sum(upstream_wide * attended.astype(F32), axis=0, keepdims=True)
    delta_pieces = split3(jnp.broadcast_to(delta, shape))
    wide_upstream = jnp.concatenate(
        [(scale * upstream_wide).astype(BF16), stacked(*delta_pieces)], axis=0
    )
    wide_value = jnp.concatenate([value, stacked(one, one, one)], axis=0)
    d_query, d_key, d_value = [], None, None
    for part in range(2):
        at = slice(part * 512, part * 512 + 512)
        weights = jnp.exp2(dot(wide_key, wide_query[:, at], TN))
        d_scores = (weights * dot(wide_value, wide_upstream[:, at], TN)).astype(BF16)
        d_query.append(dot(key, d_scores, NN))
        more_key = dot(query[:, at], d_scores, NT)
        more_value = dot(upstream[:, at], weights.astype(BF16), NT)
        d_key = more_key if d_key is None else d_key + more_key
        d_value = more_value if d_value is None else d_value + more_value
    return jnp.concatenate(d_query, axis=1).astype(BF16), d_key.astype(BF16), d_value.astype(BF16)


def attend_back_kernel(normed, qkv, bias, attended, upstream, lse, grad_out, d_qkv):
    mask = bias[...]

    def one_head(h, carry):
        d_query, d_key, d_value = backward_head(
            qkv[0, h], qkv[1, h], qkv[2, h], mask, attended[h], upstream[h], lse[h][0:1]
        )
        d_qkv[0, h] = d_query
        d_qkv[1, h] = d_key
        d_qkv[2, h] = d_value
        return carry

    lax.fori_loop(0, HEADS, one_head, 0)
    for j in range(3):
        grad = dot(d_qkv[j].reshape(256, PATCH), normed[...], NN)
        grad_out[:, j * 256 : j * 256 + 256] = grad.T.astype(BF16)


def attend_back(normed, qkv, bias, attended, upstream, lse):
    return pl.pallas_call(
        attend_back_kernel,
        out_shape=jax.ShapeDtypeStruct((D, QW), BF16),
        in_specs=[VMEM] * 6,
        out_specs=VMEM,
        scratch_shapes=[pltpu.VMEM((3, HEADS, HEAD_DIM, PATCH), BF16)],
        compiler_params=params(),
        name="attend_back",
    )(normed, qkv, bias, attended, upstream, lse)


def gelu_both(values):
    squared = values * values
    tangent = jnp.tanh(GELU_C * (values + 0.044715 * squared * values))
    half = 0.5 * (1.0 + tangent)
    derivative = half + 0.5 * values * (1.0 - tangent * tangent) * GELU_C * (
        1.0 + 3.0 * 0.044715 * squared
    )
    return values * half, derivative


CHUNK = 256


def feed_forward_kernel(
    attended, rows, upstream, proj, fc1, fc2, block_out, grad_out, d_attended_out,
    snd1, rcv1, snd2, rcv2, snd3, rcv3, own2, mixed, normed_mid, inverse, act, d_pre, d_mixed,
    send_sem, recv_sem,
):
    me, core = lax.axis_index("dp"), lax.axis_index("mp")
    sibling = (me, 1 - core)
    barrier = pltpu.get_barrier_semaphore()
    pl.semaphore_signal(barrier, inc=1, device_id=sibling, device_id_type=MESH)
    chunks = PATCH // CHUNK

    def place(i):
        return lax.rem(i + 2 * (1 - core), chunks)

    def span(k):
        return pl.ds(pl.multiple_of(k * CHUNK, CHUNK), CHUNK)

    def copy(kind, i, src, dst):
        return pltpu.make_async_remote_copy(
            src_ref=src,
            dst_ref=dst,
            send_sem=send_sem.at[kind, i],
            recv_sem=recv_sem.at[kind, i],
            device_id=sibling,
            device_id_type=MESH,
        )

    def copy1(k):
        return copy(0, k, snd1.at[span(k), :], rcv1.at[span(k), :])

    def copy2(i):
        at = pl.ds(i * CHUNK, CHUNK)
        return copy(1, i, snd2.at[at, :], rcv2.at[at, :])

    def copy3(k):
        return copy(2, k, snd3.at[span(k), :], rcv3.at[span(k), :])

    for k in range(chunks):
        partial = dot(attended[:, k * CHUNK : (k + 1) * CHUNK], proj[...], TN)
        snd1[k * CHUNK : (k + 1) * CHUNK, :] = partial.astype(BF16)
        if k == 0:
            pl.semaphore_wait(barrier, 1)
        copy1(k).start()

    for i in range(chunks):
        k = place(i)
        at = span(k)
        copy1(k).wait_recv()
        total = rows[at, :].astype(F32) + (snd1[at, :].astype(F32) + rcv1[at, :].astype(F32))
        mixed[at, :] = total
        normed, inv = normalize(total)
        inverse[at, :] = jnp.broadcast_to(inv, (CHUNK, 128))
        low = normed.astype(BF16)
        normed_mid[at, :] = low
        activation, derivative = gelu_both(dot(low, fc1[...], NN))
        act_low = activation.astype(BF16)
        act[at, :] = act_low
        partial = dot(act_low, fc2[...], NN).astype(BF16)
        if i < 2:
            snd2[i * CHUNK : (i + 1) * CHUNK, :] = partial
            copy2(i).start()
        else:
            own2[(i - 2) * CHUNK : (i - 1) * CHUNK, :] = partial
        d_low = (dot(upstream[at, :], fc2[...], NT) * derivative).astype(BF16)
        d_pre[at, :] = d_low
        snd3[at, :] = dot(d_low, fc1[...], NT).astype(BF16)
        copy3(k).start()

    for part in range(4):
        cols = slice(part * 256, part * 256 + 256)
        grad_out[:, cols] = dot(normed_mid[...], d_pre[:, cols], TN).astype(BF16)
        grad_out[:, 1024 + part * 256 : 1280 + part * 256] = dot(
            upstream[...], act[:, cols], TN
        ).astype(BF16)

    for i in range(chunks):
        k = place(i)
        at = span(k)
        copy3(k).wait_recv()
        back = snd3[at, :].astype(F32) + rcv3[at, :].astype(F32)
        inv = inverse[at, :][:, 0:1]
        total = mixed[at, :]
        center = total - jnp.mean(total, axis=-1, keepdims=True)
        normed = center * inv
        mean_grad = jnp.mean(back, axis=-1, keepdims=True)
        mean_mixed = jnp.mean(back * normed, axis=-1, keepdims=True)
        through = inv * (back - mean_grad - normed * mean_mixed)
        d_mixed[at, :] = (upstream[at, :].astype(F32) + through).astype(BF16)

    for k in range(chunks):
        at = slice(k * CHUNK, (k + 1) * CHUNK)
        d_attended_out[:, at] = dot(proj[...], d_mixed[at, :], NT).astype(BF16)
    grad_out[:, 2048:2304] = dot(attended[...], d_mixed[...], NN).T.astype(BF16)

    for i in range(2):
        copy2(i).wait_recv()
        own = slice(i * CHUNK, (i + 1) * CHUNK)
        total = mixed[span(place(i + 2)), :] + (own2[own, :].astype(F32) + rcv2[own, :].astype(F32))
        block_out[i * 32 : i * 32 + 32] = pack(total.astype(BF16).astype(F32))
    for k in range(chunks):
        copy1(k).wait_send()
        copy3(k).wait_send()
    for i in range(2):
        copy2(i).wait_send()


def feed_forward(attended, rows, upstream, proj, fc1, fc2):
    whole = pltpu.VMEM((PATCH, D), BF16)
    half = pltpu.VMEM((PATCH // 2, D), BF16)
    return pl.pallas_call(
        feed_forward_kernel,
        out_shape=(
            jax.ShapeDtypeStruct((PAIRS, 16, D // 2), BF16),
            jax.ShapeDtypeStruct((D, GW), BF16),
            jax.ShapeDtypeStruct((256, PATCH), BF16),
        ),
        in_specs=[VMEM] * 6,
        out_specs=(VMEM,) * 3,
        scratch_shapes=[
            whole,
            whole,
            half,
            half,
            whole,
            whole,
            half,
            pltpu.VMEM((PATCH, D), F32),
            whole,
            pltpu.VMEM((PATCH, 128), F32),
            pltpu.VMEM((PATCH, FF), BF16),
            pltpu.VMEM((PATCH, FF), BF16),
            whole,
            pltpu.SemaphoreType.DMA((3, 4)),
            pltpu.SemaphoreType.DMA((3, 4)),
        ],
        compiler_params=params(collective_id=2, has_side_effects=True),
        name="feed_forward",
    )(attended, rows, upstream, proj, fc1, fc2)


def axis_peers(me):
    z, x, y = lax.div(me, NX * NY), lax.rem(lax.div(me, NY), NX), lax.rem(me, NY)
    at_x = [(z * NX + lax.rem(x + d, NX)) * NY + y for d in range(NX)]
    at_z = [(lax.rem(z + d, NZ) * NX + x) * NY + y for d in range(NZ)]
    at_y = [(z * NX + x) * NY + lax.rem(y + d, NY) for d in range(NY)]
    return (z, x, y), (at_x, at_z, at_y)


class ReduceScatter:
    def __init__(self, me, core, grad, land, sems):
        self.core = core
        self.place, self.peers = axis_peers(me)
        self.grad, self.sems = grad, sems
        self.land_x, self.mid, self.land_z, self.low, self.land_y = land

    def copy(self, phase, d, src, dst):
        send, recv = self.sems
        base = (0, NX - 1, NX + NZ - 2)[phase]
        return pltpu.make_async_remote_copy(
            src_ref=src,
            dst_ref=dst,
            send_sem=send.at[base + d - 1],
            recv_sem=recv.at[base + d - 1],
            device_id=(self.peers[phase][d], self.core),
            device_id_type=MESH,
        )

    def copies(self, phase):
        z, x, _ = self.place
        if phase == 0:
            return [
                self.copy(0, d, self.grad.at[:, lax.rem(x + d, NX)], self.land_x.at[d - 1])
                for d in range(1, NX)
            ]
        if phase == 1:
            return [
                self.copy(1, d, self.mid.at[lax.rem(z + d, NZ)], self.land_z.at[d - 1])
                for d in range(1, NZ)
            ]
        return [self.copy(2, d, self.low, self.land_y.at[d - 1]) for d in range(1, NY)]

    def start(self, phase):
        for one in self.copies(phase):
            one.start()

    def arrived(self, phase):
        for one in self.copies(phase):
            one.wait_recv()

    def after_x(self):
        self.arrived(0)
        _, x, _ = self.place

        def step(i, carry):
            total = self.grad[i, x].astype(F32)
            for d in range(NX - 1):
                total = total + self.land_x[d, i].astype(F32)
            self.mid[i] = total.astype(BF16)
            return carry

        lax.fori_loop(0, NZ, step, 0)
        self.start(1)

    def after_z(self):
        self.arrived(1)
        z, _, _ = self.place
        total = self.mid[z].astype(F32)
        for d in range(NZ - 1):
            total = total + self.land_z[d].astype(F32)
        self.low[...] = total.astype(BF16)
        self.start(2)

    def after_y(self):
        self.arrived(2)
        _, _, y = self.place
        total = self.low[...].astype(F32)
        for d in range(NY - 1):
            total = total + self.land_y[d].astype(F32)
        result = total[0:4]
        for other in range(1, NY):
            result = jnp.where(y == other, total[4 * other : 4 * other + 4], result)
        return result

    def finish(self):
        for phase in range(3):
            for one in self.copies(phase):
                one.wait_send()


def reduce_scratch(columns):
    return [
        pltpu.VMEM((NX - 1, NZ, 16, columns), BF16),
        pltpu.VMEM((NZ, 16, columns), BF16),
        pltpu.VMEM((NZ - 1, 16, columns), BF16),
        pltpu.VMEM((16, columns), BF16),
        pltpu.VMEM((NY - 1, 16, columns), BF16),
        pltpu.SemaphoreType.DMA((NX + NY + NZ - 3,)),
        pltpu.SemaphoreType.DMA((NX + NY + NZ - 3,)),
    ]


def collect_kernel(block, slot, grad, grad_qkv, rows_out, sums_out, qkv_out, *scratch):
    me, core = lax.axis_index("dp"), lax.axis_index("mp")
    land, send_sem, recv_sem = scratch[:3]
    first = ReduceScatter(me, core, grad, scratch[3:8], scratch[8:10])
    second = ReduceScatter(me, core, grad_qkv, scratch[10:15], scratch[15:17])
    _, peers = axis_peers(me)
    pair_barrier(me, core, [p for axis in peers for p in axis[1:]])
    second.start(0)
    first.start(0)
    pair_sends(me, core, block, land, send_sem.at[0], recv_sem.at[0])
    second.after_x()
    first.after_x()
    second.after_z()
    first.after_z()
    pair_arrived(core, land, recv_sem.at[0])
    swap = to_sibling(me, core, land, send_sem.at[1], recv_sem.at[1])
    swap.start()
    qkv_out[...] = second.after_y()
    sums_out[...] = first.after_y()
    sibling_arrived(core, land, recv_sem.at[1])
    total = None
    for half in range(2):
        place = lax.broadcasted_iota(jnp.int32, (PATCH // 2, ROWS), 0) + half * (PATCH // 2)
        chosen = (place == slot[0:1, :]).astype(BF16)
        part = dot(chosen, unpack(land[half]).astype(BF16), TN)
        total = part if total is None else total + part
    rows_out[...] = total.astype(BF16)
    swap.wait_send()
    pair_sent(core, block, send_sem.at[0])
    first.finish()
    second.finish()


def collect(block, slot, grad, grad_qkv):
    return pl.pallas_call(
        collect_kernel,
        out_shape=(
            jax.ShapeDtypeStruct((ROWS, D), BF16),
            jax.ShapeDtypeStruct((4, GW), F32),
            jax.ShapeDtypeStruct((4, QW), F32),
        ),
        in_specs=[VMEM] * 4,
        out_specs=(VMEM,) * 3,
        scratch_shapes=[
            pltpu.VMEM((2, PAIRS, 16, D // 2), BF16),
            pltpu.SemaphoreType.DMA((2,)),
            pltpu.SemaphoreType.DMA((2,)),
            *reduce_scratch(GW),
            *reduce_scratch(QW),
        ],
        compiler_params=params(collective_id=3, has_side_effects=True),
        name="collect",
    )(block, slot, grad.reshape(NZ, NX, 16, GW), grad_qkv.reshape(NZ, NX, 16, QW))


def per_device(points, patch_of, qkv_weight, proj_weight, fc1_weight, fc2_weight, cotangent):
    weight = qkv_weight.reshape(D, QW).T
    rows, upstream, bias, slot = dispatch(points, cotangent, patch_of.reshape(1, ROWS))
    normed, qkv, attended, lse = attend(rows, weight, bias)
    block, grad, d_attended = feed_forward(
        attended.reshape(256, PATCH), rows, upstream, proj_weight, fc1_weight, fc2_weight
    )
    grad_qkv = attend_back(
        normed, qkv, bias, attended, d_attended.reshape(HEADS, HEAD_DIM, PATCH), lse
    )
    block_out, sums, qkv_sums = collect(block, slot, grad, grad_qkv)
    return (
        block_out,
        qkv_sums.reshape(4, 3, 256),
        sums[:, 2048:2304].T,
        sums[:, :1024],
        sums[:, 1024:2048].T,
    )


def solution(mesh):
    placed = (
        P("dp", None),
        P("dp", None),
        P(None, None, "mp"),
        P("mp", None),
        P(None, "mp"),
        P("mp", None),
        P("dp", None),
    )
    return jax.shard_map(
        per_device,
        mesh=mesh,
        in_specs=placed,
        out_specs=(P("dp", None), P("dp", None, "mp"), P("mp", "dp"), P("dp", "mp"), P("mp", "dp")),
        check_vma=False,
    )
```

time: 608 us -> 212 us (0.35); the launches traced: 599 us -> 210 us
  waiting for transfers between devices: 323 us -> 0 us
  Pallas kernels: 0 us -> 201 us
  matrix products: 129 us -> 0 us
  local copies, waits for them, and re-layouts: 54.5 us -> 8.09 us
  starting transfers between devices: 46 us -> 0 us
  other arithmetic: 31.2 us -> 0 us
  between operations: 15.1 us -> 0.66 us
    unnamed x4 -> x0, waiting for transfers between devices: 208 us -> none
    pallas_call x0 -> x5, Pallas kernels: none -> 201 us  [the longest x1 69.4 us: collect(): pl.pallas_call(collect_kernel, out_shape=(jax.ShapeDtypeStruct((ROWS, D),...]
    dot_general x39 -> x0, matrix products: 129 us -> none  [the longest x4 29.1 us: one_group(): jnp.einsum('qhd,khd->hqk', group_grad, group_value, preferred_element_typ...]
    all_to_all x4 -> x0, waiting for transfers between devices: 74.4 us -> none  [the longest x1 39.8 us: per_device(): lax.all_to_all(block_rows.reshape(sources, bucket, features), 'dp', split...]
    all_to_all x4 -> x0, starting transfers between devices: 45.7 us -> none  [the longest x1 16.3 us: per_device(): lax.all_to_all(send_flags, 'dp', split_axis=0, concat_axis=0, tiled=True)]
    psum x2 -> x0, waiting for transfers between devices: 40.6 us -> none  [the longest x1 23.9 us: per_device(): lax.psum(partial_mlp.astype(jnp.bfloat16), 'mp').astype(jnp.float32)]
    while x8 -> x0, local copies, waits for them, and re-layouts: 22.9 us -> none
    reduce_sum x10 -> x0, other arithmetic: 22.6 us -> none  [the longest x4 16 us: one_group(): totals = jnp.sum(exponent, axis=2, keepdims=True)]
  transfers between devices with their start and end apart: 7 -> 0, of which waited for: 7 -> 0; matrix products, arithmetic and copies ran while one was open for 4% -> 0% of each run, Pallas kernels for 0% -> 0%
where the time goes in v1:
time: 212 us; the launch traced here: 210 us
  Pallas kernels  201 us (95%)
  local copies, waits for them, and re-layouts  8.09 us (4%)
    pallas_call x1, Pallas kernels, collect(): pl.pallas_call(collect_kernel, out_shape=(jax.ShapeDtypeStruct((ROWS, D),...  69.4 us
    pallas_call x1, Pallas kernels, attend_back(): pl.pallas_call(attend_back_kernel, out_shape=jax.ShapeDtypeStruct((D, QW)...  46 us
    pallas_call x1, Pallas kernels, dispatch(): pl.pallas_call(dispatch_kernel, out_shape=(jax.ShapeDtypeStruct((PATCH, D...  43.8 us
    pallas_call x1, Pallas kernels, attend(): pl.pallas_call(attend_kernel, out_shape=(jax.ShapeDtypeStruct((PATCH, D),...  24.6 us
    pallas_call x1, Pallas kernels, feed_forward(): pl.pallas_call(feed_forward_kernel, out_shape=(jax.ShapeDtypeStruct((PAIR...  17.6 us
    unnamed x3, local copies, waits for them, and re-layouts  5.48 us

profile of v1, /device:TPU:1, one launch (start us, length us, event | category | flops | bytes accessed | tf_op | source)
XLA Modules:
  0.0 210.2 jit_solution(14166800477295808324)
XLA Ops:
  0.6 2.3 %copy.14 = bf16[512,3,256]{0,2,1:T(8,128)(2,1)} copy(bf16[512,3,256]{2,0,1:T(8,128)(2,1)} %param.9) | data formatting | bytes 1572864 | tf_op args[2]
  2.9 43.8 %dispatch.1 = (bf16[1024,512]{1,0:T(8,128)(2,1)}, bf16[1024,512]{1,0:T(8,128)(2,1)}, bf16[16,1024]{1,0:T(8,128)(2,1)}, s32[8,512]{1,0:T(8,128)}) custom-call(bf16[512,512]{1,0:T(8,128)(2,1)} %points.1, bf16[512,512]{1,0:T(8,128)(2,1)} %cotangent.1, s32[1,512]{1,0:T(1,128)} %bitcast.19), custom_call_target="tpu_custom_call" | custom-call | tf_op jit(solution)/shard_map/dispatch/pallas_call | solution.py:212
  46.7 24.6 %attend.1 = (bf16[1024,512]{1,0:T(8,128)(2,1)}, bf16[3,16,16,1024]{3,2,1,0:T(8,128)(2,1)}, bf16[16,16,1024]{2,1,0:T(8,128)(2,1)}, f32[16,8,1024]{2,1,0:T(8,128)}) custom-call(bf16[1024,512]{1,0:T(8,128)(2,1)} %get-tuple-element.19.rows, bf16[768,512]{1,0:T(8,128)(2,1)} %bitcast.14, bf16[16,1024]{1,0:T(8,128)(2,1)} %get-tuple-element.20.bias), custom_call_target="tpu_custom_call" | custom-call | tf_op jit(solution)/shard_map/attend/pallas_call | solution.py:270
  71.3 17.6 %feed_forward.1 = (bf16[64,16,256]{2,1,0:T(8,128)(2,1)}, bf16[512,2304]{1,0:T(8,128)(2,1)}, bf16[256,1024]{1,0:T(8,128)(2,1)}) custom-call(bf16[256,1024]{1,0:T(8,128)(2,1)} %bitcast.16, bf16[1024,512]{1,0:T(8,128)(2,1)} %get-tuple-element.19.rows, bf16[1024,512]{1,0:T(8,128)(2,1)} %get-tuple-element.22.upstream, bf16[256,512]{1,0:T(8,128)(2,1)} %proj.1, ...), custom_call_target="tpu_custom_call" | custom-call | tf_op jit(solution)/shard_map/feed_forward/pallas_call | solution.py:474
  88.9 46.0 %attend_back.1 = bf16[512,768]{1,0:T(8,128)(2,1)} custom-call(bf16[1024,512]{1,0:T(8,128)(2,1)} %get-tuple-element.26.normed, bf16[3,16,16,1024]{3,2,1,0:T(8,128)(2,1)} %get-tuple-element.27.qkv, bf16[16,1024]{1,0:T(8,128)(2,1)} %get-tuple-element.20.bias, bf16[16,16,1024]{2,1,0:T(8,128)(2,1)} %get-tuple-element.21.attended, bf16[16,16,1024]{2,1,0:T(8,128)(2,1)} %bitcast.17, ...), custom_call_target="tpu_custom_call" | custom-call | tf_op jit(solution)/shard_map/attend_back/pallas_call | solution.py:341
  135.0 69.4 %collect.1 = (bf16[512,512]{1,0:T(8,128)(2,1)}, f32[4,2304]{1,0:T(4,128)}, f32[4,768]{1,0:T(4,128)}) custom-call(bf16[64,16,256]{2,1,0:T(8,128)(2,1)} %get-tuple-element.23.block, s32[8,512]{1,0:T(8,128)} %get-tuple-element.24.slot, bf16[8,4,16,2304]{3,2,1,0:T(8,128)(2,1)} %bitcast.15, bf16[8,4,16,768]{3,2,1,0:T(8,128)(2,1)} %bitcast.13), custom_call_target="tpu_custom_call" | custom-call | tf_op jit(solution)/shard_map/collect/pallas_call | solution.py:640
  204.4 1.3 slice_bitcast_fusion.1
  205.6 1.3 slice_bitcast_fusion
  207.0 1.9 copy.17
  208.8 1.3 copy.18

commit v2 on v1

--- a/solution.py
+++ b/solution.py
@@ -26,8 +26,11 @@
 MASKED = -1e30
 NX, NY, NZ = 4, 4, 8
 PAIRS = 64
-GW = 2304
-QW = 768
+FIRST_HEADS = 12
+AW = 1280
+BW = 1024
+QA = 3 * HEAD_DIM * FIRST_HEADS
+QB = 3 * HEAD_DIM * (HEADS - FIRST_HEADS)
 
 
 def dot(left, right, dims):
@@ -309,44 +312,14 @@
     d_query, d_key, d_value = [], None, None
     for part in range(2):
         at = slice(part * 512, part * 512 + 512)
-        weights = jnp.exp2(dot(wide_key, wide_query[:, at], TN))
-        d_scores = (weights * dot(wide_value, wide_upstream[:, at], TN)).astype(BF16)
-        d_query.append(dot(key, d_scores, NN))
-        more_key = dot(query[:, at], d_scores, NT)
-        more_value = dot(upstream[:, at], weights.astype(BF16), NT)
+        weights = jnp.exp2(dot(wide_query[:, at], wide_key, TN))
+        d_scores = (weights * dot(wide_upstream[:, at], wide_value, TN)).astype(BF16)
+        d_query.append(dot(key, d_scores, NT))
+        more_key = dot(query[:, at], d_scores, NN)
+        more_value = dot(upstream[:, at], weights.astype(BF16), NN)
         d_key = more_key if d_key is None else d_key + more_key
         d_value = more_value if d_value is None else d_value + more_value
     return jnp.concatenate(d_query, axis=1).astype(BF16), d_key.astype(BF16), d_value.astype(BF16)
-
-
-def attend_back_kernel(normed, qkv, bias, attended, upstream, lse, grad_out, d_qkv):
-    mask = bias[...]
-
-    def one_head(h, carry):
-        d_query, d_key, d_value = backward_head(
-            qkv[0, h], qkv[1, h], qkv[2, h], mask, attended[h], upstream[h], lse[h][0:1]
-        )
-        d_qkv[0, h] = d_query
-        d_qkv[1, h] = d_key
-        d_qkv[2, h] = d_value
-        return carry
-
-    lax.fori_loop(0, HEADS, one_head, 0)
-    for j in range(3):
-        grad = dot(d_qkv[j].reshape(256, PATCH), normed[...], NN)
-        grad_out[:, j * 256 : j * 256 + 256] = grad.T.astype(BF16)
-
-
-def attend_back(normed, qkv, bias, attended, upstream, lse):
-    return pl.pallas_call(
-        attend_back_kernel,
-        out_shape=jax.ShapeDtypeStruct((D, QW), BF16),
-        in_specs=[VMEM] * 6,
-        out_specs=VMEM,
-        scratch_shapes=[pltpu.VMEM((3, HEADS, HEAD_DIM, PATCH), BF16)],
-        compiler_params=params(),
-        name="attend_back",
-    )(normed, qkv, bias, attended, upstream, lse)
 
 
 def gelu_both(values):
@@ -362,9 +335,17 @@
 CHUNK = 256
 
 
+def row_order():
+    place = lax.broadcasted_iota(jnp.int32, (D, D), 1)
+    y, z, x, j = place >> 7, (place >> 4) & 7, (place >> 2) & 3, place & 3
+    channel = (z << 6) + (x << 4) + (y << 2) + j
+    return (lax.broadcasted_iota(jnp.int32, (D, D), 0) == channel).astype(BF16)
+
+
 def feed_forward_kernel(
-    attended, rows, upstream, proj, fc1, fc2, block_out, grad_out, d_attended_out,
+    attended, rows, upstream, proj, fc1, fc2, block_out, grad_a, grad_b, d_attended_out,
     snd1, rcv1, snd2, rcv2, snd3, rcv3, own2, mixed, normed_mid, inverse, act, d_pre, d_mixed,
+    permuted,
     send_sem, recv_sem,
 ):
     me, core = lax.axis_index("dp"), lax.axis_index("mp")
@@ -430,12 +411,11 @@
         snd3[at, :] = dot(d_low, fc1[...], NT).astype(BF16)
         copy3(k).start()
 
+    permuted[...] = dot(upstream[...], row_order(), NN).astype(BF16)
     for part in range(4):
         cols = slice(part * 256, part * 256 + 256)
-        grad_out[:, cols] = dot(normed_mid[...], d_pre[:, cols], TN).astype(BF16)
-        grad_out[:, 1024 + part * 256 : 1280 + part * 256] = dot(
-            upstream[...], act[:, cols], TN
-        ).astype(BF16)
+        grad_a[:, cols] = dot(normed_mid[...], d_pre[:, cols], TN).astype(BF16)
+        grad_b[:, cols] = dot(permuted[...], act[:, cols], TN).astype(BF16)
 
     for i in range(chunks):
         k = place(i)
@@ -454,7 +434,7 @@
     for k in range(chunks):
         at = slice(k * CHUNK, (k + 1) * CHUNK)
         d_attended_out[:, at] = dot(proj[...], d_mixed[at, :], NT).astype(BF16)
-    grad_out[:, 2048:2304] = dot(attended[...], d_mixed[...], NN).T.astype(BF16)
+    grad_a[:, 1024:1280] = dot(attended[...], d_mixed[...], NN).T.astype(BF16)
 
     for i in range(2):
         copy2(i).wait_recv()
@@ -475,11 +455,12 @@
         feed_forward_kernel,
         out_shape=(
             jax.ShapeDtypeStruct((PAIRS, 16, D // 2), BF16),
-            jax.ShapeDtypeStruct((D, GW), BF16),
+            jax.ShapeDtypeStruct((D, AW), BF16),
+            jax.ShapeDtypeStruct((D, BW), BF16),
             jax.ShapeDtypeStruct((256, PATCH), BF16),
         ),
         in_specs=[VMEM] * 6,
-        out_specs=(VMEM,) * 3,
+        out_specs=(VMEM,) * 4,
         scratch_shapes=[
             whole,
             whole,
@@ -494,6 +475,7 @@
             pltpu.VMEM((PATCH, FF), BF16),
             pltpu.VMEM((PATCH, FF), BF16),
             whole,
+            whole,
             pltpu.SemaphoreType.DMA((3, 4)),
             pltpu.SemaphoreType.DMA((3, 4)),
         ],
@@ -502,48 +484,45 @@
     )(attended, rows, upstream, proj, fc1, fc2)
 
 
-def axis_peers(me):
-    z, x, y = lax.div(me, NX * NY), lax.rem(lax.div(me, NY), NX), lax.rem(me, NY)
-    at_x = [(z * NX + lax.rem(x + d, NX)) * NY + y for d in range(NX)]
-    at_z = [(lax.rem(z + d, NZ) * NX + x) * NY + y for d in range(NZ)]
-    at_y = [(z * NX + x) * NY + lax.rem(y + d, NY) for d in range(NY)]
-    return (z, x, y), (at_x, at_z, at_y)
-
-
 class ReduceScatter:
-    def __init__(self, me, core, grad, land, sems):
-        self.core = core
-        self.place, self.peers = axis_peers(me)
-        self.grad, self.sems = grad, sems
-        self.land_x, self.mid, self.land_z, self.low, self.land_y = land
+    def __init__(self, me, core, x_first, grad, scratch):
+        z, x, y = lax.div(me, NX * NY), lax.rem(lax.div(me, NY), NX), lax.rem(me, NY)
+        at_x = [(z * NX + lax.rem(x + d, NX)) * NY + y for d in range(NX)]
+        at_z = [(lax.rem(z + d, NZ) * NX + x) * NY + y for d in range(NZ)]
+        at_y = [(z * NX + x) * NY + lax.rem(y + d, NY) for d in range(NY)]
+        self.core, self.x_first = core, x_first
+        self.peers = (at_x, at_z, at_y) if x_first else (at_y, at_z, at_x)
+        self.place = (x, z, y) if x_first else (y, z, x)
+        self.grad = grad
+        self.land_0, self.mid, self.land_1, self.low, self.land_2, self.send, self.recv = scratch
 
     def copy(self, phase, d, src, dst):
-        send, recv = self.sems
         base = (0, NX - 1, NX + NZ - 2)[phase]
         return pltpu.make_async_remote_copy(
             src_ref=src,
             dst_ref=dst,
-            send_sem=send.at[base + d - 1],
-            recv_sem=recv.at[base + d - 1],
+            send_sem=self.send.at[base + d - 1],
+            recv_sem=self.recv.at[base + d - 1],
             device_id=(self.peers[phase][d], self.core),
             device_id_type=MESH,
         )
 
+    def piece(self, d):
+        at = lax.rem(self.place[0] + d, NX)
+        return self.grad.at[:, at] if self.x_first else self.grad.at[at]
+
     def copies(self, phase):
-        z, x, _ = self.place
         if phase == 0:
+            return [self.copy(0, d, self.piece(d), self.land_0.at[d - 1]) for d in range(1, NX)]
+        if phase == 1:
+            z = self.place[1]
             return [
-                self.copy(0, d, self.grad.at[:, lax.rem(x + d, NX)], self.land_x.at[d - 1])
-                for d in range(1, NX)
-            ]
-        if phase == 1:
-            return [
-                self.copy(1, d, self.mid.at[lax.rem(z + d, NZ)], self.land_z.at[d - 1])
+                self.copy(1, d, self.mid.at[lax.rem(z + d, NZ)], self.land_1.at[d - 1])
                 for d in range(1, NZ)
             ]
-        return [self.copy(2, d, self.low, self.land_y.at[d - 1]) for d in range(1, NY)]
-
-    def start(self, phase):
+        return [self.copy(2, d, self.low, self.land_2.at[d - 1]) for d in range(1, NY)]
+
+    def start(self, phase=0):
         for one in self.copies(phase):
             one.start()
 
@@ -551,38 +530,38 @@
         for one in self.copies(phase):
             one.wait_recv()
 
-    def after_x(self):
+    def second(self):
         self.arrived(0)
-        _, x, _ = self.place
+        mine = self.place[0]
 
         def step(i, carry):
-            total = self.grad[i, x].astype(F32)
+            own = self.grad[i, mine] if self.x_first else self.grad[mine, i]
+            total = own.astype(F32)
             for d in range(NX - 1):
-                total = total + self.land_x[d, i].astype(F32)
+                total = total + self.land_0[d, i].astype(F32)
             self.mid[i] = total.astype(BF16)
             return carry
 
         lax.fori_loop(0, NZ, step, 0)
         self.start(1)
 
-    def after_z(self):
+    def third(self):
         self.arrived(1)
-        z, _, _ = self.place
-        total = self.mid[z].astype(F32)
+        total = self.mid[self.place[1]].astype(F32)
         for d in range(NZ - 1):
-            total = total + self.land_z[d].astype(F32)
+            total = total + self.land_1[d].astype(F32)
         self.low[...] = total.astype(BF16)
         self.start(2)
 
-    def after_y(self):
+    def result(self):
         self.arrived(2)
-        _, _, y = self.place
         total = self.low[...].astype(F32)
         for d in range(NY - 1):
-            total = total + self.land_y[d].astype(F32)
+            total = total + self.land_2[d].astype(F32)
         result = total[0:4]
         for other in range(1, NY):
-            result = jnp.where(y == other, total[4 * other : 4 * other + 4], result)
+            part = total[4 * other : 4 * other + 4]
+            result = jnp.where(self.place[2] == other, part, result)
         return result
 
     def finish(self):
@@ -603,26 +582,120 @@
     ]
 
 
-def collect_kernel(block, slot, grad, grad_qkv, rows_out, sums_out, qkv_out, *scratch):
+def attend_back_kernel(
+    block, grad_a, grad_b, normed, qkv, bias, attended, upstream, lse,
+    land, sums_a, sums_b, sums_qa, sums_qb,
+    d_qkv, grad_qa, grad_qb, send_sem, recv_sem, *scratch,
+):
     me, core = lax.axis_index("dp"), lax.axis_index("mp")
-    land, send_sem, recv_sem = scratch[:3]
-    first = ReduceScatter(me, core, grad, scratch[3:8], scratch[8:10])
-    second = ReduceScatter(me, core, grad_qkv, scratch[10:15], scratch[15:17])
-    _, peers = axis_peers(me)
-    pair_barrier(me, core, [p for axis in peers for p in axis[1:]])
-    second.start(0)
-    first.start(0)
+    parts = [
+        ReduceScatter(me, core, first, grad, scratch[7 * i : 7 * i + 7])
+        for i, (first, grad) in enumerate(
+            ((True, grad_a), (False, grad_b), (True, grad_qa), (True, grad_qb))
+        )
+    ]
+    part_a, part_b, part_qa, part_qb = parts
+    swap = to_sibling(me, core, land, send_sem.at[1], recv_sem.at[1])
+    pair_barrier(me, core, [p for axis in part_a.peers for p in axis[1:]])
+    part_a.start()
+    part_b.start()
     pair_sends(me, core, block, land, send_sem.at[0], recv_sem.at[0])
-    second.after_x()
-    first.after_x()
-    second.after_z()
-    first.after_z()
-    pair_arrived(core, land, recv_sem.at[0])
-    swap = to_sibling(me, core, land, send_sem.at[1], recv_sem.at[1])
-    swap.start()
-    qkv_out[...] = second.after_y()
-    sums_out[...] = first.after_y()
+    mask = bias[...]
+
+    def project(first, last, out):
+        rows = (last - first) * HEAD_DIM
+        heads = [d_qkv[j, first:last].reshape(rows, PATCH) for j in range(3)]
+        grad = dot(jnp.concatenate(heads, axis=0), normed[...], NN)
+        out[...] = grad.T.astype(BF16).reshape(out.shape)
+
+    def one_head(h, carry):
+        @pl.when(h == 6)
+        def _():
+            part_a.second()
+            part_b.second()
+
+        @pl.when(h == 11)
+        def _():
+            part_a.third()
+            part_b.third()
+
+        @pl.when(h == FIRST_HEADS)
+        def _():
+            project(0, FIRST_HEADS, grad_qa)
+            part_qa.start()
+            pair_arrived(core, land, recv_sem.at[0])
+            swap.start()
+
+        @pl.when(h == 15)
+        def _():
+            part_qa.second()
+
+        d_query, d_key, d_value = backward_head(
+            qkv[0, h], qkv[1, h], qkv[2, h], mask, attended[h], upstream[h], lse[h][0:1]
+        )
+        d_qkv[0, h] = d_query
+        d_qkv[1, h] = d_key
+        d_qkv[2, h] = d_value
+        return carry
+
+    lax.fori_loop(0, HEADS, one_head, 0)
+    project(FIRST_HEADS, HEADS, grad_qb)
+    part_qb.start()
+    part_qa.third()
+    sums_a[...] = part_a.result()
+    sums_b[...] = part_b.result()
+    part_qb.second()
     sibling_arrived(core, land, recv_sem.at[1])
+    part_qb.third()
+    sums_qa[...] = part_qa.result()
+    swap.wait_send()
+    pair_sent(core, block, send_sem.at[0])
+    sums_qb[...] = part_qb.result()
+    for part in parts:
+        part.finish()
+
+
+def attend_back(block, grad_a, grad_b, normed, qkv, bias, attended, upstream, lse):
+    return pl.pallas_call(
+        attend_back_kernel,
+        out_shape=(
+            jax.ShapeDtypeStruct((2, PAIRS, 16, D // 2), BF16),
+            jax.ShapeDtypeStruct((4, AW), F32),
+            jax.ShapeDtypeStruct((4, BW), F32),
+            jax.ShapeDtypeStruct((4, QA), F32),
+            jax.ShapeDtypeStruct((4, QB), F32),
+        ),
+        in_specs=[VMEM] * 9,
+        out_specs=(VMEM,) * 5,
+        scratch_shapes=[
+            pltpu.VMEM((3, HEADS, HEAD_DIM, PATCH), BF16),
+            pltpu.VMEM((NZ, NX, 16, QA), BF16),
+            pltpu.VMEM((NZ, NX, 16, QB), BF16),
+            pltpu.SemaphoreType.DMA((2,)),
+            pltpu.SemaphoreType.DMA((2,)),
+            *reduce_scratch(AW),
+            *reduce_scratch(BW),
+            *reduce_scratch(QA),
+            *reduce_scratch(QB),
+        ],
+        compiler_params=params(collective_id=3, has_side_effects=True),
+        name="attend_back",
+    )(
+        block,
+        grad_a.reshape(NZ, NX, 16, AW),
+        grad_b.reshape(NY, NZ, 16, BW),
+        normed,
+        qkv,
+        bias,
+        attended,
+        upstream,
+        lse,
+    )
+
+
+def finish_kernel(
+    land, slot, sums_a, sums_b, sums_qa, sums_qb, rows_out, qkv_out, proj_out, fc1_out, fc2_out
+):
     total = None
     for half in range(2):
         place = lax.broadcasted_iota(jnp.int32, (PATCH // 2, ROWS), 0) + half * (PATCH // 2)
@@ -630,52 +703,52 @@
         part = dot(chosen, unpack(land[half]).astype(BF16), TN)
         total = part if total is None else total + part
     rows_out[...] = total.astype(BF16)
-    swap.wait_send()
-    pair_sent(core, block, send_sem.at[0])
-    first.finish()
-    second.finish()
-
-
-def collect(block, slot, grad, grad_qkv):
+
+    def turned(rows):
+        return jnp.concatenate([rows, rows], axis=0).T[:, 0:4]
+
+    fc1_out[...] = sums_a[:, :FF]
+    proj_out[...] = turned(sums_a[:, FF:])
+    fc2_out[...] = turned(sums_b[...])
+    first, last = sums_qa[...], sums_qb[...]
+    n, m = QA // 3, QB // 3
+    for j in range(3):
+        both = jnp.concatenate(
+            [first[:, j * n : (j + 1) * n], last[:, j * m : (j + 1) * m]], axis=1
+        )
+        for i in range(4):
+            qkv_out[i, j : j + 1, :] = both[i : i + 1, :]
+
+
+def finish(*given):
     return pl.pallas_call(
-        collect_kernel,
+        finish_kernel,
         out_shape=(
             jax.ShapeDtypeStruct((ROWS, D), BF16),
-            jax.ShapeDtypeStruct((4, GW), F32),
-            jax.ShapeDtypeStruct((4, QW), F32),
+            jax.ShapeDtypeStruct((4, 3, 256), F32),
+            jax.ShapeDtypeStruct((256, 4), F32),
+            jax.ShapeDtypeStruct((4, FF), F32),
+            jax.ShapeDtypeStruct((FF, 4), F32),
         ),
-        in_specs=[VMEM] * 4,
-        out_specs=(VMEM,) * 3,
-        scratch_shapes=[
-            pltpu.VMEM((2, PAIRS, 16, D // 2), BF16),
-            pltpu.SemaphoreType.DMA((2,)),
-            pltpu.SemaphoreType.DMA((2,)),
-            *reduce_scratch(GW),
-            *reduce_scratch(QW),
-        ],
-        compiler_params=params(collective_id=3, has_side_effects=True),
-        name="collect",
-    )(block, slot, grad.reshape(NZ, NX, 16, GW), grad_qkv.reshape(NZ, NX, 16, QW))
+        in_specs=[VMEM] * 6,
+        out_specs=(VMEM,) * 5,
+        compiler_params=params(),
+        name="finish",
+    )(*given)
 
 
 def per_device(points, patch_of, qkv_weight, proj_weight, fc1_weight, fc2_weight, cotangent):
-    weight = qkv_weight.reshape(D, QW).T
+    weight = qkv_weight.reshape(D, 3 * 256).T
     rows, upstream, bias, slot = dispatch(points, cotangent, patch_of.reshape(1, ROWS))
     normed, qkv, attended, lse = attend(rows, weight, bias)
-    block, grad, d_attended = feed_forward(
+    block, grad_a, grad_b, d_attended = feed_forward(
         attended.reshape(256, PATCH), rows, upstream, proj_weight, fc1_weight, fc2_weight
     )
-    grad_qkv = attend_back(
-        normed, qkv, bias, attended, d_attended.reshape(HEADS, HEAD_DIM, PATCH), lse
+    d_attended = d_attended.reshape(HEADS, HEAD_DIM, PATCH)
+    land, *sums = attend_back(
+        block, grad_a, grad_b, normed, qkv, bias, attended, d_attended, lse
     )
-    block_out, sums, qkv_sums = collect(block, slot, grad, grad_qkv)
-    return (
-        block_out,
-        qkv_sums.reshape(4, 3, 256),
-        sums[:, 2048:2304].T,
-        sums[:, :1024],
-        sums[:, 1024:2048].T,
-    )
+    return tuple(finish(land, slot, *sums))
 
 
 def solution(mesh):

time: 212 us -> 174 us (0.82)
  Pallas kernels: 201 us -> 165 us
    pallas_call x2, Pallas kernels: 115 us -> 78.5 us  [the longest x1 75.5 us: attend_back(): pl.pallas_call(attend_back_kernel, out_shape=(jax.ShapeDtypeStruct((2, PA...]
    pallas_call x0 -> x3, local copies, waits for them, and re-layouts: none -> 4.73 us  [finish(): pl.pallas_call(finish_kernel, out_shape=(jax.ShapeDtypeStruct((ROWS, D),...]
    unnamed x3 -> x1, local copies, waits for them, and re-layouts: 5.48 us -> 2.31 us
    transpose x2 -> x0, local copies, waits for them, and re-layouts: 2.61 us -> none  [the longest x1 1.35 us: per_device(): sums[:, 1024:2048]]
where the time goes in v2:
time: 174 us; the launch traced here: 173 us
  Pallas kernels  165 us (95%)
  local copies, waits for them, and re-layouts  7.04 us (4%)
    pallas_call x1, Pallas kernels, attend_back(): pl.pallas_call(attend_back_kernel, out_shape=(jax.ShapeDtypeStruct((2, PA...  75.5 us
    pallas_call x1, Pallas kernels, dispatch(): pl.pallas_call(dispatch_kernel, out_shape=(jax.ShapeDtypeStruct((PATCH, D...  43.7 us
    pallas_call x1, Pallas kernels, attend(): pl.pallas_call(attend_kernel, out_shape=(jax.ShapeDtypeStruct((PATCH, D),...  24.6 us
    pallas_call x1, Pallas kernels, feed_forward(): pl.pallas_call(feed_forward_kernel, out_shape=(jax.ShapeDtypeStruct((PAIR...  18.1 us
    pallas_call x3, local copies, waits for them, and re-layouts, finish(): pl.pallas_call(finish_kernel, out_shape=(jax.ShapeDtypeStruct((ROWS, D),...  4.73 us

profile of v2, /device:TPU:1, one launch (start us, length us, event | category | flops | bytes accessed | tf_op | source)
XLA Modules:
  0.0 172.7 jit_solution(1402214200869141480)
XLA Ops:
  0.6 2.3 %copy.12 = bf16[512,3,256]{0,2,1:T(8,128)(2,1)} copy(bf16[512,3,256]{2,0,1:T(8,128)(2,1)} %param.9) | data formatting | bytes 1572864 | tf_op args[2]
  2.9 43.7 %dispatch.1 = (bf16[1024,512]{1,0:T(8,128)(2,1)}, bf16[1024,512]{1,0:T(8,128)(2,1)}, bf16[16,1024]{1,0:T(8,128)(2,1)}, s32[8,512]{1,0:T(8,128)}) custom-call(bf16[512,512]{1,0:T(8,128)(2,1)} %points.1, bf16[512,512]{1,0:T(8,128)(2,1)} %cotangent.1, s32[1,512]{1,0:T(1,128)} %bitcast.13), custom_call_target="tpu_custom_call" | custom-call | tf_op jit(solution)/shard_map/dispatch/pallas_call | solution.py:215
  46.7 24.6 %attend.1 = (bf16[1024,512]{1,0:T(8,128)(2,1)}, bf16[3,16,16,1024]{3,2,1,0:T(8,128)(2,1)}, bf16[16,16,1024]{2,1,0:T(8,128)(2,1)}, f32[16,8,1024]{2,1,0:T(8,128)}) custom-call(bf16[1024,512]{1,0:T(8,128)(2,1)} %get-tuple-element.22.rows, bf16[768,512]{1,0:T(8,128)(2,1)} %bitcast.8, bf16[16,1024]{1,0:T(8,128)(2,1)} %get-tuple-element.23.bias), custom_call_target="tpu_custom_call" | custom-call | tf_op jit(solution)/shard_map/attend/pallas_call | solution.py:273
  71.3 18.1 %feed_forward.1 = (bf16[64,16,256]{2,1,0:T(8,128)(2,1)}, bf16[512,1280]{1,0:T(8,128)(2,1)}, bf16[512,1024]{1,0:T(8,128)(2,1)}, bf16[256,1024]{1,0:T(8,128)(2,1)}) custom-call(bf16[256,1024]{1,0:T(8,128)(2,1)} %bitcast.9, bf16[1024,512]{1,0:T(8,128)(2,1)} %get-tuple-element.22.rows, bf16[1024,512]{1,0:T(8,128)(2,1)} %get-tuple-element.25.upstream, ...), custom_call_target="tpu_custom_call" | custom-call | tf_op jit(solution)/shard_map/feed_forward/pallas_call | solution.py:454
  89.5 75.5 %attend_back.1 = (bf16[2,64,16,256]{3,2,1,0:T(8,128)(2,1)}, f32[4,1280]{1,0:T(4,128)}, f32[4,1024]{1,0:T(4,128)}, f32[4,576]{1,0:T(4,128)}, f32[4,192]{1,0:T(4,128)}) custom-call(bf16[64,16,256]{2,1,0:T(8,128)(2,1)} %get-tuple-element.26.block, bf16[8,4,16,1280]{3,2,1,0:T(8,128)(2,1)} %bitcast.10, bf16[4,8,16,1024]{3,2,1,0:T(8,128)(2,1)} %bitcast.11, ...), custom_call_target="tpu_custom_call" | custom-call | tf_op jit(solution)/shard_map/attend_back/pallas_call | solution.py:659
  164.9 3.0 %finish.1 = (bf16[512,512]{1,0:T(8,128)(2,1)}, f32[4,3,256]{2,1,0:T(4,128)}, f32[256,4]{1,0:T(8,128)}, f32[4,1024]{1,0:T(4,128)}, f32[1024,4]{1,0:T(8,128)}) custom-call(bf16[2,64,16,256]{3,2,1,0:T(8,128)(2,1)} %get-tuple-element.33.land, s32[8,512]{1,0:T(8,128)} %get-tuple-element.34.slot, f32[4,1280]{1,0:T(4,128)} %get-tuple-element.35.sums_a, ...), custom_call_target="tpu_custom_call" | custom-call | tf_op jit(solution)/shard_map/finish/pallas_call | solution.py:724
  168.0 1.6 copy.14
  169.5 1.3 copy.13
  170.9 1.8 %copy.15 = f32[1024,4]{0,1:T(4,128)} copy(f32[1024,4]{1,0:T(8,128)} %get-tuple-element.43) | data formatting | bytes 32768 | tf_op jit(solution)/shard_map/finish/pallas_call | solution.py:724

commit v3 on v2

v3 whole, which is shorter than its diff:
```python
import math
import types

import jax
import jax.numpy as jnp
from jax import lax
from jax.experimental import pallas as pl
from jax.experimental.pallas import tpu as pltpu
from jax.sharding import PartitionSpec as P

MESH = pl.DeviceIdType.MESH
F32 = jnp.float32
BF16 = jnp.bfloat16
VMEM = pl.BlockSpec(memory_space=pltpu.VMEM)

HEADS = 16
HEAD_DIM = 16
PATCH = 1024
ROWS = 512
D = 512
FF = 1024
EPS = 1e-05
GELU_C = math.sqrt(2.0 / math.pi)
EXP2_SCALE = HEAD_DIM**-0.5 * math.log2(math.e)
EMPTY = 64.0
MASKED = -1e30
NX, NY, NZ = 4, 4, 8
PAIRS = 64
FIRST_HEADS = 12
AW = 1280
BW = 1024
QA = 3 * HEAD_DIM * FIRST_HEADS
QB = 3 * HEAD_DIM * (HEADS - FIRST_HEADS)


def dot(left, right, dims):
    return lax.dot_general(left, right, (dims, ((), ())), preferred_element_type=F32)


NN = ((1,), (0,))
NT = ((1,), (1,))
TN = ((0,), (0,))


def params(**more):
    return pltpu.CompilerParams(vmem_limit_bytes=60 << 20, **more)


def normalize(values):
    center = values - jnp.mean(values, axis=-1, keepdims=True)
    inverse = lax.rsqrt(jnp.mean(center * center, axis=-1, keepdims=True) + EPS)
    return center * inverse, inverse


def split3(x):
    a = x.astype(BF16)
    r = x - a.astype(F32)
    b = r.astype(BF16)
    return a, b, (r - b.astype(F32)).astype(BF16)


def pack(rows):
    n = rows.shape[0] // 8
    pieces = rows.reshape(n, 8, D)
    return jnp.concatenate([pieces[:, :, : D // 2], pieces[:, :, D // 2 :]], axis=1).astype(BF16)


def unpack(pieces):
    wide = pieces.astype(F32)
    n = wide.shape[0]
    return jnp.concatenate([wide[:, :8], wide[:, 8:]], axis=2).reshape(8 * n, D)


def pair_greet(me, core, extra=()):
    barrier = pltpu.get_barrier_semaphore()
    parity = lax.rem(core + me, 2)

    def greet(i, carry):
        other = 2 * lax.rem(lax.div(me, 2) + i, PAIRS) + parity
        pl.semaphore_signal(barrier, inc=1, device_id=(other, core), device_id_type=MESH)
        return carry

    lax.fori_loop(1, PAIRS, greet, 0)

    @pl.when(core == 1)
    def _():
        other = 2 * lax.div(me, 2) + parity
        pl.semaphore_signal(barrier, inc=1, device_id=(other, core), device_id_type=MESH)

    pl.semaphore_signal(barrier, inc=1, device_id=(me, 1 - core), device_id_type=MESH)
    for other in extra:
        pl.semaphore_signal(barrier, inc=1, device_id=(other, core), device_id_type=MESH)


def pair_greeted(core, extra=()):
    pl.semaphore_wait(pltpu.get_barrier_semaphore(), PAIRS + core + len(extra))


def pair_sends(me, core, out, landing, send_sem, recv_sem):
    parity = lax.rem(core + me, 2)
    mine = lax.div(me, 2)

    def push(place):
        pltpu.make_async_remote_copy(
            src_ref=out.at[place],
            dst_ref=landing.at[core, mine],
            send_sem=send_sem,
            recv_sem=recv_sem,
            device_id=(2 * place + parity, core),
            device_id_type=MESH,
        ).start()

    @pl.when(core == 0)
    def _():
        pltpu.make_async_copy(out.at[mine], landing.at[core, mine], recv_sem).start()

    @pl.when(core == 1)
    def _():
        push(mine)

    def step(i, carry):
        push(lax.rem(mine + i, PAIRS))
        return carry

    lax.fori_loop(1, PAIRS, step, 0)


def pair_arrived(core, landing, recv_sem):
    pltpu.make_async_copy(landing.at[core], landing.at[core], recv_sem).wait()


def pair_sent(core, out, send_sem):
    most = out.at[pl.ds(0, PAIRS - 1)]
    pltpu.make_async_copy(most, most, send_sem).wait()

    @pl.when(core == 1)
    def _():
        pltpu.make_async_copy(out.at[0], out.at[0], send_sem).wait()


def to_sibling(me, core, landing, send_sem, recv_sem):
    return pltpu.make_async_remote_copy(
        src_ref=landing.at[core],
        dst_ref=landing.at[core],
        send_sem=send_sem,
        recv_sem=recv_sem,
        device_id=(me, 1 - core),
        device_id_type=MESH,
    )


def sibling_arrived(core, landing, recv_sem):
    pltpu.make_async_copy(landing.at[1 - core], landing.at[1 - core], recv_sem).wait()


def slot_rows(patch, me):
    member = (lax.broadcasted_iota(jnp.int32, (128, ROWS), 0) == patch).astype(BF16)
    before = (
        lax.broadcasted_iota(jnp.int32, (ROWS, ROWS), 0)
        < lax.broadcasted_iota(jnp.int32, (ROWS, ROWS), 1)
    ).astype(BF16)
    earlier = dot(member, before, NN)
    within = jnp.sum(earlier * member.astype(F32), axis=0, keepdims=True).astype(jnp.int32)
    return ((patch + me) & 1) * (PATCH // 2) + (patch >> 1) * 8 + within


def forward_head(query, key, value, bias):
    scaled = split3(query.astype(F32) * EXP2_SCALE)
    wide_query = jnp.concatenate([*scaled, jnp.ones((16, PATCH), BF16)], axis=0)
    wide_key = jnp.concatenate([key, key, key, bias], axis=0)
    scores = dot(wide_key, wide_query, TN)
    maxima = jnp.max(scores, axis=0, keepdims=True)
    weights = jnp.exp2(scores - maxima)
    totals = jnp.sum(weights, axis=0, keepdims=True)
    result = dot(value, weights.astype(BF16), NN) / totals
    return result.astype(BF16), maxima + jnp.log2(totals)


def dispatch_and_attend(me, core, ref, others):
    pair_greet(me, core, others)
    slot = slot_rows(ref.patch[...], me)
    ref.slot_out[...] = jnp.broadcast_to(slot, (8, ROWS))
    place = lax.broadcasted_iota(jnp.int32, (PATCH // 2, ROWS), 0) + core * (PATCH // 2)
    chosen = (place == slot).astype(BF16)
    filled = dot(chosen, jnp.ones((ROWS, 128), BF16), NN)
    fill = EMPTY * (1.0 - jnp.concatenate([filled] * (D // 128), axis=1))
    ref.out_p[...] = pack(dot(chosen, ref.points[...], NN) + fill)
    pair_greeted(core, others)
    send, recv = ref.pair_send, ref.pair_recv
    pair_sends(me, core, ref.out_p, ref.land_p, send.at[0], recv.at[0])
    ref.out_c[...] = pack(dot(chosen, ref.cotangent[...], NN))
    swap_p = to_sibling(me, core, ref.land_p, send.at[2], recv.at[2])
    swap_c = to_sibling(me, core, ref.land_c, send.at[3], recv.at[3])
    pair_arrived(core, ref.land_p, recv.at[0])
    swap_p.start()
    pair_sends(me, core, ref.out_c, ref.land_c, send.at[1], recv.at[1])
    ones = jnp.ones((16, 128), BF16)

    def receive(half):
        for part in range(2):
            start = pl.multiple_of(half * 512 + part * 256, 256)
            at = pl.ds(start, 256)
            wide = unpack(ref.land_p[half, part * 32 : part * 32 + 32])
            empty = wide > 0.5 * EMPTY
            real = jnp.where(empty, 0.0, wide)
            ref.rows[at, :] = real.astype(BF16)
            count = dot(ones, jnp.where(empty[:, :128], 1.0, 0.0).astype(BF16), NT)
            first_row = lax.broadcasted_iota(jnp.int32, (16, 256), 0) == 0
            ref.bias[:, at] = jnp.where(first_row & (count > 0.5), MASKED, 0.0).astype(BF16)
            normed = normalize(real)[0].astype(BF16)
            ref.normed[at, :] = normed
            for j in range(3):
                projected = dot(ref.weight[j], normed, ((0,), (1,))).astype(BF16)
                ref.qkv[j, :, :, at] = projected.reshape(HEADS, HEAD_DIM, 256)

    receive(core)
    sibling_arrived(core, ref.land_p, recv.at[2])
    receive(1 - core)
    mask = ref.bias[...]

    def pair(i, carry):
        @pl.when(i == 6)
        def _():
            pair_arrived(core, ref.land_c, recv.at[1])
            swap_c.start()

        for u in range(2):
            h = 2 * i + u
            result, lse = forward_head(ref.qkv[0, h], ref.qkv[1, h], ref.qkv[2, h], mask)
            ref.attended[h] = result
            ref.lse[h] = jnp.broadcast_to(lse, (8, PATCH))
        return carry

    lax.fori_loop(0, HEADS // 2, pair, 0)

    def upstream_arrived():
        sibling_arrived(core, ref.land_c, recv.at[3])
        for half in range(2):
            for part in range(2):
                at = half * 512 + part * 256
                pieces = ref.land_c[half, part * 32 : part * 32 + 32]
                ref.upstream[at : at + 256, :] = unpack(pieces).astype(BF16)

    def finish():
        swap_p.wait_send()
        swap_c.wait_send()
        pair_sent(core, ref.out_p, send.at[0])
        pair_sent(core, ref.out_c, send.at[1])

    return upstream_arrived, finish


def backward_head(query, key, value, bias, attended, upstream, lse):
    shape = (16, PATCH)
    row = lax.broadcasted_iota(jnp.int32, shape, 0)
    one = jnp.ones(shape, BF16)
    zero = jnp.zeros(shape, BF16)

    def stacked(*given):
        total = zero
        for at, value_at in enumerate(given):
            total = jnp.where(row == at, value_at, total)
        return total

    lse_pieces = split3(-jnp.broadcast_to(lse, shape))
    scaled = split3(query.astype(F32) * EXP2_SCALE)
    wide_query = jnp.concatenate([*scaled, stacked(one, *lse_pieces)], axis=0)
    wide_key = jnp.concatenate([key, key, key, stacked(bias, one, one, one)], axis=0)
    scale = HEAD_DIM**-0.5
    upstream_wide = upstream.astype(F32)
    delta = -scale * jnp.sum(upstream_wide * attended.astype(F32), axis=0, keepdims=True)
    delta_pieces = split3(jnp.broadcast_to(delta, shape))
    wide_upstream = jnp.concatenate(
        [(scale * upstream_wide).astype(BF16), stacked(*delta_pieces)], axis=0
    )
    wide_value = jnp.concatenate([value, stacked(one, one, one)], axis=0)
    d_query, d_key, d_value = [], None, None
    for part in range(2):
        at = slice(part * 512, part * 512 + 512)
        weights = jnp.exp2(dot(wide_query[:, at], wide_key, TN))
        d_scores = (weights * dot(wide_upstream[:, at], wide_value, TN)).astype(BF16)
        d_query.append(dot(key, d_scores, NT))
        more_key = dot(query[:, at], d_scores, NN)
        more_value = dot(upstream[:, at], weights.astype(BF16), NN)
        d_key = more_key if d_key is None else d_key + more_key
        d_value = more_value if d_value is None else d_value + more_value
    return jnp.concatenate(d_query, axis=1).astype(BF16), d_key.astype(BF16), d_value.astype(BF16)


def gelu_both(values):
    squared = values * values
    tangent = jnp.tanh(GELU_C * (values + 0.044715 * squared * values))
    half = 0.5 * (1.0 + tangent)
    derivative = half + 0.5 * values * (1.0 - tangent * tangent) * GELU_C * (
        1.0 + 3.0 * 0.044715 * squared
    )
    return values * half, derivative


CHUNK = 256


def row_order():
    place = lax.broadcasted_iota(jnp.int32, (D, D), 1)
    y, z, x, j = place >> 7, (place >> 4) & 7, (place >> 2) & 3, place & 3
    channel = (z << 6) + (x << 4) + (y << 2) + j
    return (lax.broadcasted_iota(jnp.int32, (D, D), 0) == channel).astype(BF16)


def feed_forward(me, core, ref, upstream_arrived, part_a, part_b):
    sibling = (me, 1 - core)
    chunks = PATCH // CHUNK
    proj, fc1, fc2 = ref.proj, ref.fc1, ref.fc2

    def place(i):
        return lax.rem(i + 2 * (1 - core), chunks)

    def span(k):
        return pl.ds(pl.multiple_of(k * CHUNK, CHUNK), CHUNK)

    def copy(kind, i, src, dst):
        return pltpu.make_async_remote_copy(
            src_ref=src,
            dst_ref=dst,
            send_sem=ref.core_send.at[kind, i],
            recv_sem=ref.core_recv.at[kind, i],
            device_id=sibling,
            device_id_type=MESH,
        )

    def copy1(k):
        return copy(0, k, ref.snd1.at[span(k), :], ref.rcv1.at[span(k), :])

    def copy2(i):
        at = pl.ds(i * CHUNK, CHUNK)
        return copy(1, i, ref.snd2.at[at, :], ref.rcv2.at[at, :])

    def copy3(k):
        return copy(2, k, ref.snd3.at[span(k), :], ref.rcv3.at[span(k), :])

    for i in range(chunks):
        k = place(i)
        heads = ref.attended[:, :, span(k)].reshape(256, CHUNK)
        ref.snd1[span(k), :] = dot(heads, proj[...], TN).astype(BF16)
        copy1(k).start()
    upstream_arrived()

    for i in range(chunks):
        k = place(i)
        at = span(k)
        copy1(k).wait_recv()
        added = ref.snd1[at, :].astype(F32) + ref.rcv1[at, :].astype(F32)
        total = ref.rows[at, :].astype(F32) + added
        ref.mixed[at, :] = total
        normed, inv = normalize(total)
        ref.inverse[at, :] = jnp.broadcast_to(inv, (CHUNK, 128))
        low = normed.astype(BF16)
        ref.normed_mid[at, :] = low
        activation, derivative = gelu_both(dot(low, fc1[...], NN))
        act_low = activation.astype(BF16)
        ref.act[at, :] = act_low
        partial = dot(act_low, fc2[...], NN).astype(BF16)
        if i < 2:
            ref.snd2[i * CHUNK : (i + 1) * CHUNK, :] = partial
            copy2(i).start()
        else:
            ref.own2[(i - 2) * CHUNK : (i - 1) * CHUNK, :] = partial
        d_low = (dot(ref.upstream[at, :], fc2[...], NT) * derivative).astype(BF16)
        ref.d_pre[at, :] = d_low
        ref.snd3[at, :] = dot(d_low, fc1[...], NT).astype(BF16)
        copy3(k).start()

    ref.permuted[...] = dot(ref.upstream[...], row_order(), NN).astype(BF16)
    for part in range(4):
        cols = slice(part * 256, part * 256 + 256)
        grad = dot(ref.permuted[...], ref.act[:, cols], TN).astype(BF16)
        ref.grad_b[:, :, :, cols] = grad.reshape(NY, NZ, 16, 256)
    part_b.start()
    for part in range(4):
        cols = slice(part * 256, part * 256 + 256)
        grad = dot(ref.normed_mid[...], ref.d_pre[:, cols], TN).astype(BF16)
        ref.grad_a[:, :, :, cols] = grad.reshape(NZ, NX, 16, 256)

    for i in range(chunks):
        k = place(i)
        at = span(k)
        copy3(k).wait_recv()
        back = ref.snd3[at, :].astype(F32) + ref.rcv3[at, :].astype(F32)
        inv = ref.inverse[at, :][:, 0:1]
        total = ref.mixed[at, :]
        center = total - jnp.mean(total, axis=-1, keepdims=True)
        normed = center * inv
        mean_grad = jnp.mean(back, axis=-1, keepdims=True)
        mean_mixed = jnp.mean(back * normed, axis=-1, keepdims=True)
        through = inv * (back - mean_grad - normed * mean_mixed)
        low = (ref.upstream[at, :].astype(F32) + through).astype(BF16)
        ref.d_mixed[at, :] = low
        heads = dot(proj[...], low, NT).astype(BF16)
        ref.d_attended[:, :, at] = heads.reshape(HEADS, HEAD_DIM, CHUNK)

    grad = dot(ref.attended[...].reshape(256, PATCH), ref.d_mixed[...], NN).T.astype(BF16)
    ref.grad_a[:, :, :, FF:AW] = grad.reshape(NZ, NX, 16, AW - FF)
    part_a.start()

    for i in range(2):
        copy2(i).wait_recv()
        own = slice(i * CHUNK, (i + 1) * CHUNK)
        added = ref.own2[own, :].astype(F32) + ref.rcv2[own, :].astype(F32)
        total = ref.mixed[span(place(i + 2)), :] + added
        ref.block[i * 32 : i * 32 + 32] = pack(total.astype(BF16).astype(F32))

    def finish():
        for k in range(chunks):
            copy1(k).wait_send()
            copy3(k).wait_send()
        for i in range(2):
            copy2(i).wait_send()

    return finish


class ReduceScatter:
    def __init__(self, me, core, x_first, grad, scratch):
        z, x, y = lax.div(me, NX * NY), lax.rem(lax.div(me, NY), NX), lax.rem(me, NY)
        at_x = [(z * NX + lax.rem(x + d, NX)) * NY + y for d in range(NX)]
        at_z = [(lax.rem(z + d, NZ) * NX + x) * NY + y for d in range(NZ)]
        at_y = [(z * NX + x) * NY + lax.rem(y + d, NY) for d in range(NY)]
        self.core, self.x_first = core, x_first
        self.peers = (at_x, at_z, at_y) if x_first else (at_y, at_z, at_x)
        self.place = (x, z, y) if x_first else (y, z, x)
        self.grad = grad
        self.land_0, self.mid, self.land_1, self.low, self.land_2, self.send, self.recv = scratch

    def copy(self, phase, d, src, dst):
        base = (0, NX - 1, NX + NZ - 2)[phase]
        return pltpu.make_async_remote_copy(
            src_ref=src,
            dst_ref=dst,
            send_sem=self.send.at[base + d - 1],
            recv_sem=self.recv.at[base + d - 1],
            device_id=(self.peers[phase][d], self.core),
            device_id_type=MESH,
        )

    def piece(self, d):
        at = lax.rem(self.place[0] + d, NX)
        return self.grad.at[:, at] if self.x_first else self.grad.at[at]

    def copies(self, phase):
        if phase == 0:
            return [self.copy(0, d, self.piece(d), self.land_0.at[d - 1]) for d in range(1, NX)]
        if phase == 1:
            z = self.place[1]
            return [
                self.copy(1, d, self.mid.at[lax.rem(z + d, NZ)], self.land_1.at[d - 1])
                for d in range(1, NZ)
            ]
        return [self.copy(2, d, self.low, self.land_2.at[d - 1]) for d in range(1, NY)]

    def start(self, phase=0):
        for one in self.copies(phase):
            one.start()

    def arrived(self, phase):
        for one in self.copies(phase):
            one.wait_recv()

    def second(self):
        self.arrived(0)
        mine = self.place[0]

        def step(i, carry):
            own = self.grad[i, mine] if self.x_first else self.grad[mine, i]
            total = own.astype(F32)
            for d in range(NX - 1):
                total = total + self.land_0[d, i].astype(F32)
            self.mid[i] = total.astype(BF16)
            return carry

        lax.fori_loop(0, NZ, step, 0)
        self.start(1)

    def third(self):
        self.arrived(1)
        total = self.mid[self.place[1]].astype(F32)
        for d in range(NZ - 1):
            total = total + self.land_1[d].astype(F32)
        self.low[...] = total.astype(BF16)
        self.start(2)

    def result(self):
        self.arrived(2)
        total = self.low[...].astype(F32)
        for d in range(NY - 1):
            total = total + self.land_2[d].astype(F32)
        result = total[0:4]
        for other in range(1, NY):
            part = total[4 * other : 4 * other + 4]
            result = jnp.where(self.place[2] == other, part, result)
        return result

    def finish(self):
        for phase in range(3):
            for one in self.copies(phase):
                one.wait_send()


def reduce_scratch(columns):
    return [
        pltpu.VMEM((NX - 1, NZ, 16, columns), BF16),
        pltpu.VMEM((NZ, 16, columns), BF16),
        pltpu.VMEM((NZ - 1, 16, columns), BF16),
        pltpu.VMEM((16, columns), BF16),
        pltpu.VMEM((NY - 1, 16, columns), BF16),
        pltpu.SemaphoreType.DMA((NX + NY + NZ - 3,)),
        pltpu.SemaphoreType.DMA((NX + NY + NZ - 3,)),
    ]


SCRATCH = dict(
    out_p=((PAIRS, 16, D // 2), BF16),
    out_c=((PAIRS, 16, D // 2), BF16),
    land_p=((2, PAIRS, 16, D // 2), BF16),
    land_c=((2, PAIRS, 16, D // 2), BF16),
    rows=((PATCH, D), BF16),
    upstream=((PATCH, D), BF16),
    bias=((16, PATCH), BF16),
    normed=((PATCH, D), BF16),
    qkv=((3, HEADS, HEAD_DIM, PATCH), BF16),
    attended=((HEADS, HEAD_DIM, PATCH), BF16),
    lse=((HEADS, 8, PATCH), F32),
    snd1=((PATCH, D), BF16),
    rcv1=((PATCH, D), BF16),
    snd2=((PATCH // 2, D), BF16),
    rcv2=((PATCH // 2, D), BF16),
    own2=((PATCH // 2, D), BF16),
    snd3=((PATCH, D), BF16),
    rcv3=((PATCH, D), BF16),
    mixed=((PATCH, D), F32),
    normed_mid=((PATCH, D), BF16),
    inverse=((PATCH, 128), F32),
    act=((PATCH, FF), BF16),
    d_pre=((PATCH, FF), BF16),
    d_mixed=((PATCH, D), BF16),
    permuted=((PATCH, D), BF16),
    d_attended=((HEADS, HEAD_DIM, PATCH), BF16),
    block=((PAIRS, 16, D // 2), BF16),
    d_qkv=((3, HEADS, HEAD_DIM, PATCH), BF16),
    grad_a=((NZ, NX, 16, AW), BF16),
    grad_b=((NY, NZ, 16, BW), BF16),
    grad_qa=((NZ, NX, 16, QA), BF16),
    grad_qb=((NZ, NX, 16, QB), BF16),
)
SEMAPHORES = dict(pair_send=(6,), pair_recv=(6,), core_send=(3, 4), core_recv=(3, 4))
INPUTS = ("points", "cotangent", "patch", "weight", "proj", "fc1", "fc2")
OUTPUTS = ("land", "slot_out", "sums_a", "sums_b", "sums_qa", "sums_qb")


def block_kernel(*refs):
    names = (*INPUTS, *OUTPUTS, *SCRATCH, *SEMAPHORES)
    ref = types.SimpleNamespace(**dict(zip(names, refs)))
    rest = refs[len(names) :]
    me, core = lax.axis_index("dp"), lax.axis_index("mp")
    parts = [
        ReduceScatter(me, core, first, grad, rest[7 * i : 7 * i + 7])
        for i, (first, grad) in enumerate(
            ((True, ref.grad_a), (False, ref.grad_b), (True, ref.grad_qa), (True, ref.grad_qb))
        )
    ]
    part_a, part_b, part_qa, part_qb = parts
    others = [p for axis in part_a.peers for p in axis[1:]]
    upstream_arrived, finish_attend = dispatch_and_attend(me, core, ref, others)
    finish_feed = feed_forward(me, core, ref, upstream_arrived, part_a, part_b)
    land, block, d_qkv = ref.land, ref.block, ref.d_qkv
    send, recv = ref.pair_send, ref.pair_recv
    pair_sends(me, core, block, land, send.at[4], recv.at[4])
    swap = to_sibling(me, core, land, send.at[5], recv.at[5])
    finish_attend()
    mask = ref.bias[...]

    def project(first, last, out):
        rows = (last - first) * HEAD_DIM
        heads = [d_qkv[j, first:last].reshape(rows, PATCH) for j in range(3)]
        grad = dot(jnp.concatenate(heads, axis=0), ref.normed[...], NN)
        out[...] = grad.T.astype(BF16).reshape(out.shape)

    def pair(i, carry):
        @pl.when(i == 5)
        def _():
            part_a.second()
            part_b.second()

        @pl.when(i == FIRST_HEADS // 2)
        def _():
            project(0, FIRST_HEADS, ref.grad_qa)
            part_qa.start()
            pair_arrived(core, land, recv.at[4])
            swap.start()

        for u in range(2):
            h = 2 * i + u
            d_query, d_key, d_value = backward_head(
                ref.qkv[0, h], ref.qkv[1, h], ref.qkv[2, h], mask,
                ref.attended[h], ref.d_attended[h], ref.lse[h][0:1],
            )
            d_qkv[0, h] = d_query
            d_qkv[1, h] = d_key
            d_qkv[2, h] = d_value
        return carry

    lax.fori_loop(0, HEADS // 2, pair, 0)
    project(FIRST_HEADS, HEADS, ref.grad_qb)
    part_qb.start()
    part_a.third()
    part_b.third()
    part_qa.second()
    part_qb.second()
    ref.sums_a[...] = part_a.result()
    ref.sums_b[...] = part_b.result()
    part_qa.third()
    part_qb.third()
    sibling_arrived(core, land, recv.at[5])
    swap.wait_send()
    pair_sent(core, block, send.at[4])
    finish_feed()
    ref.sums_qa[...] = part_qa.result()
    ref.sums_qb[...] = part_qb.result()
    for part in parts:
        part.finish()


def whole_block(*given):
    return pl.pallas_call(
        block_kernel,
        out_shape=(
            jax.ShapeDtypeStruct((2, PAIRS, 16, D // 2), BF16),
            jax.ShapeDtypeStruct((8, ROWS), jnp.int32),
            jax.ShapeDtypeStruct((4, AW), F32),
            jax.ShapeDtypeStruct((4, BW), F32),
            jax.ShapeDtypeStruct((4, QA), F32),
            jax.ShapeDtypeStruct((4, QB), F32),
        ),
        in_specs=[VMEM] * len(INPUTS),
        out_specs=(VMEM,) * len(OUTPUTS),
        scratch_shapes=[
            *(pltpu.VMEM(*shape) for shape in SCRATCH.values()),
            *(pltpu.SemaphoreType.DMA(shape) for shape in SEMAPHORES.values()),
            *reduce_scratch(AW),
            *reduce_scratch(BW),
            *reduce_scratch(QA),
            *reduce_scratch(QB),
        ],
        compiler_params=params(collective_id=1, has_side_effects=True),
        name="block",
    )(*given)


def finish_kernel(
    land, slot, sums_a, sums_b, sums_qa, sums_qb, rows_out, qkv_out, proj_out, fc1_out, fc2_out
):
    total = None
    for half in range(2):
        place = lax.broadcasted_iota(jnp.int32, (PATCH // 2, ROWS), 0) + half * (PATCH // 2)
        chosen = (place == slot[0:1, :]).astype(BF16)
        part = dot(chosen, unpack(land[half]).astype(BF16), TN)
        total = part if total is None else total + part
    rows_out[...] = total.astype(BF16)

    fc1_out[...] = sums_a[:, :FF]
    proj_out[...] = sums_a[:, FF:]
    fc2_out[...] = sums_b[...]
    first, last = sums_qa[...], sums_qb[...]
    n, m = QA // 3, QB // 3
    for j in range(3):
        qkv_out[j, :, :n] = first[:, j * n : (j + 1) * n]
        qkv_out[j, :, n:] = last[:, j * m : (j + 1) * m]


def finish(*given):
    return pl.pallas_call(
        finish_kernel,
        out_shape=(
            jax.ShapeDtypeStruct((ROWS, D), BF16),
            jax.ShapeDtypeStruct((3, 4, 256), F32),
            jax.ShapeDtypeStruct((4, 256), F32),
            jax.ShapeDtypeStruct((4, FF), F32),
            jax.ShapeDtypeStruct((4, FF), F32),
        ),
        in_specs=[VMEM] * 6,
        out_specs=(VMEM,) * 5,
        compiler_params=params(),
        name="finish",
    )(*given)


def per_device(points, patch_of, qkv_weight, proj_weight, fc1_weight, fc2_weight, cotangent):
    landed = whole_block(
        points,
        cotangent,
        patch_of.reshape(1, ROWS),
        qkv_weight.transpose(1, 0, 2),
        proj_weight,
        fc1_weight,
        fc2_weight,
    )
    block_out, grad_qkv, grad_proj, grad_fc1, grad_fc2 = finish(*landed)
    return block_out, grad_qkv.transpose(1, 0, 2), grad_proj.T, grad_fc1, grad_fc2.T


def solution(mesh):
    placed = (
        P("dp", None),
        P("dp", None),
        P(None, None, "mp"),
        P("mp", None),
        P(None, "mp"),
        P("mp", None),
        P("dp", None),
    )
    return jax.shard_map(
        per_device,
        mesh=mesh,
        in_specs=placed,
        out_specs=(P("dp", None), P("dp", None, "mp"), P("mp", "dp"), P("dp", "mp"), P("mp", "dp")),
        check_vma=False,
    )
```

time: 174 us -> 128 us (0.74)
  Pallas kernels: 165 us -> 128 us
  local copies, waits for them, and re-layouts: 7.04 us -> 0 us
    pallas_call x4 -> x1, Pallas kernels: 162 us -> 125 us  [whole_block(): pl.pallas_call(block_kernel, out_shape=(jax.ShapeDtypeStruct((2, PAIRS, 1...]
    pallas_call x3 -> x0, local copies, waits for them, and re-layouts: 4.73 us -> none  [finish(): pl.pallas_call(finish_kernel, out_shape=(jax.ShapeDtypeStruct((ROWS, D),...]
    unnamed x1 -> x0, local copies, waits for them, and re-layouts: 2.31 us -> none
where the time goes in v3:
time: 128 us
  Pallas kernels  128 us (100%)
    pallas_call x1, Pallas kernels, whole_block(): pl.pallas_call(block_kernel, out_shape=(jax.ShapeDtypeStruct((2, PAIRS, 1...  125 us
    pallas_call x1, Pallas kernels, finish(): pl.pallas_call(finish_kernel, out_shape=(jax.ShapeDtypeStruct((ROWS, D),...  2.82 us

profile of v3, /device:TPU:1, one launch (start us, length us, event | category | flops | bytes accessed | tf_op | source)
XLA Modules:
  0.0 128.3 jit_solution(10551038158606926029)
XLA Ops:
  0.6 124.9 %block.1 = (bf16[2,64,16,256]{3,2,1,0:T(8,128)(2,1)}, s32[8,512]{1,0:T(8,128)}, f32[4,1280]{1,0:T(4,128)}, f32[4,1024]{1,0:T(4,128)}, f32[4,576]{1,0:T(4,128)}, /*index=5*/f32[4,192]{1,0:T(4,128)}) custom-call(bf16[512,512]{1,0:T(8,128)(2,1)} %refs_0_.1, bf16[512,512]{1,0:T(8,128)(2,1)} %refs_1_.1, s32[1,512]{1,0:T(1,128)} %bitcast.6, ...), custom_call_target="tpu_custom_call" | custom-call | tf_op jit(solution)/shard_map/block/pallas_call | solution.py:633
  125.5 2.8 %finish.1 = (bf16[512,512]{1,0:T(8,128)(2,1)}, f32[3,4,256]{2,1,0:T(4,128)}, f32[4,256]{1,0:T(4,128)}, f32[4,1024]{1,0:T(4,128)}, f32[4,1024]{1,0:T(4,128)}) custom-call(bf16[2,64,16,256]{3,2,1,0:T(8,128)(2,1)} %get-tuple-element.16.land, s32[8,512]{1,0:T(8,128)} %get-tuple-element.17.slot, f32[4,1280]{1,0:T(4,128)} %get-tuple-element.18.sums_a, ...), custom_call_target="tpu_custom_call" | custom-call | tf_op jit(solution)/shard_map/finish/pallas_call | solution.py:680

commit v4 on v3

--- a/solution.py
+++ b/solution.py
@@ -26,6 +26,7 @@
 MASKED = -1e30
 NX, NY, NZ = 4, 4, 8
 PAIRS = 64
+SECOND = 5
 FIRST_HEADS = 12
 AW = 1280
 BW = 1024
@@ -96,14 +97,20 @@
     pl.semaphore_wait(pltpu.get_barrier_semaphore(), PAIRS + core + len(extra))
 
 
-def pair_sends(me, core, out, landing, send_sem, recv_sem):
+def offset(i):
+    return lax.rem(i * 11, PAIRS)
+
+
+def pair_sends(me, core, out, landing, send_sem, recv_sems, back=False):
     parity = lax.rem(core + me, 2)
     mine = lax.div(me, 2)
 
-    def push(place):
+    def push(i, recv_sem):
+        distance = PAIRS - offset(i) if back else offset(i)
+        place = lax.rem(mine + distance, PAIRS)
         pltpu.make_async_remote_copy(
-            src_ref=out.at[place],
-            dst_ref=landing.at[core, mine],
+            src_ref=out.at[i if back else place],
+            dst_ref=landing.at[core, mine if back else i],
             send_sem=send_sem,
             recv_sem=recv_sem,
             device_id=(2 * place + parity, core),
@@ -112,21 +119,25 @@
 
     @pl.when(core == 0)
     def _():
-        pltpu.make_async_copy(out.at[mine], landing.at[core, mine], recv_sem).start()
+        own = landing.at[core, mine if back else 0]
+        pltpu.make_async_copy(out.at[0 if back else mine], own, recv_sems[0]).start()
 
     @pl.when(core == 1)
     def _():
-        push(mine)
-
-    def step(i, carry):
-        push(lax.rem(mine + i, PAIRS))
-        return carry
-
-    lax.fori_loop(1, PAIRS, step, 0)
-
-
-def pair_arrived(core, landing, recv_sem):
-    pltpu.make_async_copy(landing.at[core], landing.at[core], recv_sem).wait()
+        push(0, recv_sems[0])
+
+    each = PAIRS // len(recv_sems)
+    for k, recv_sem in enumerate(recv_sems):
+
+        def step(i, carry, recv_sem=recv_sem):
+            push(i, recv_sem)
+            return carry
+
+        lax.fori_loop(max(1, k * each), (k + 1) * each, step, 0)
+
+
+def pair_arrived(landed, recv_sem):
+    pltpu.make_async_copy(landed, landed, recv_sem).wait()
 
 
 def pair_sent(core, out, send_sem):
@@ -138,19 +149,15 @@
         pltpu.make_async_copy(out.at[0], out.at[0], send_sem).wait()
 
 
-def to_sibling(me, core, landing, send_sem, recv_sem):
+def to_sibling(me, core, landed, send_sem, recv_sem):
     return pltpu.make_async_remote_copy(
-        src_ref=landing.at[core],
-        dst_ref=landing.at[core],
+        src_ref=landed,
+        dst_ref=landed,
         send_sem=send_sem,
         recv_sem=recv_sem,
         device_id=(me, 1 - core),
         device_id_type=MESH,
     )
-
-
-def sibling_arrived(core, landing, recv_sem):
-    pltpu.make_async_copy(landing.at[1 - core], landing.at[1 - core], recv_sem).wait()
 
 
 def slot_rows(patch, me):
@@ -177,9 +184,10 @@
 
 
 def dispatch_and_attend(me, core, ref, others):
+    for load in ref.loads:
+        load.start()
     pair_greet(me, core, others)
     slot = slot_rows(ref.patch[...], me)
-    ref.slot_out[...] = jnp.broadcast_to(slot, (8, ROWS))
     place = lax.broadcasted_iota(jnp.int32, (PATCH // 2, ROWS), 0) + core * (PATCH // 2)
     chosen = (place == slot).astype(BF16)
     filled = dot(chosen, jnp.ones((ROWS, 128), BF16), NN)
@@ -187,41 +195,55 @@
     ref.out_p[...] = pack(dot(chosen, ref.points[...], NN) + fill)
     pair_greeted(core, others)
     send, recv = ref.pair_send, ref.pair_recv
-    pair_sends(me, core, ref.out_p, ref.land_p, send.at[0], recv.at[0])
+    pair_sends(me, core, ref.out_p, ref.land_p, send.at[0], (recv.at[0], recv.at[6]))
     ref.out_c[...] = pack(dot(chosen, ref.cotangent[...], NN))
-    swap_p = to_sibling(me, core, ref.land_p, send.at[2], recv.at[2])
-    swap_c = to_sibling(me, core, ref.land_c, send.at[3], recv.at[3])
-    pair_arrived(core, ref.land_p, recv.at[0])
-    swap_p.start()
-    pair_sends(me, core, ref.out_c, ref.land_c, send.at[1], recv.at[1])
+    ref.order_b[...] = row_order(lambda y, z, x: (y, z, x), (NY, NZ, NX))
+    ref.order_q[...] = row_order(lambda x, y, z: (y, z, x), (NX, NY, NZ))
+
+    def landed(half, part):
+        return ref.land_p.at[half, pl.ds(part * 32, 32)]
+
+    swaps = [
+        to_sibling(me, core, landed(core, part), send.at[2 + 4 * part], recv.at[2 + 5 * part])
+        for part in range(2)
+    ]
+    swap_c = to_sibling(me, core, ref.land_c.at[core], send.at[3], recv.at[3])
     ones = jnp.ones((16, 128), BF16)
 
-    def receive(half):
-        for part in range(2):
-            start = pl.multiple_of(half * 512 + part * 256, 256)
-            at = pl.ds(start, 256)
-            wide = unpack(ref.land_p[half, part * 32 : part * 32 + 32])
-            empty = wide > 0.5 * EMPTY
-            real = jnp.where(empty, 0.0, wide)
-            ref.rows[at, :] = real.astype(BF16)
-            count = dot(ones, jnp.where(empty[:, :128], 1.0, 0.0).astype(BF16), NT)
-            first_row = lax.broadcasted_iota(jnp.int32, (16, 256), 0) == 0
-            ref.bias[:, at] = jnp.where(first_row & (count > 0.5), MASKED, 0.0).astype(BF16)
-            normed = normalize(real)[0].astype(BF16)
-            ref.normed[at, :] = normed
-            for j in range(3):
-                projected = dot(ref.weight[j], normed, ((0,), (1,))).astype(BF16)
-                ref.qkv[j, :, :, at] = projected.reshape(HEADS, HEAD_DIM, 256)
-
-    receive(core)
-    sibling_arrived(core, ref.land_p, recv.at[2])
-    receive(1 - core)
+    def receive(half, part):
+        start = pl.multiple_of(half * 512 + part * 256, 256)
+        at = pl.ds(start, 256)
+        wide = unpack(ref.land_p[half, part * 32 : part * 32 + 32])
+        empty = wide > 0.5 * EMPTY
+        real = jnp.where(empty, 0.0, wide)
+        ref.rows[at, :] = real.astype(BF16)
+        count = dot(ones, jnp.where(empty[:, :128], 1.0, 0.0).astype(BF16), NT)
+        first_row = lax.broadcasted_iota(jnp.int32, (16, 256), 0) == 0
+        ref.bias[:, at] = jnp.where(first_row & (count > 0.5), MASKED, 0.0).astype(BF16)
+        normed = normalize(real)[0].astype(BF16)
+        ref.normed[at, :] = normed
+        for j in range(3):
+            projected = dot(ref.weight[j], normed, ((0,), (1,))).astype(BF16)
+            ref.qkv[j, :, :, at] = projected.reshape(HEADS, HEAD_DIM, 256)
+
+    for load in ref.loads:
+        load.wait()
+    pair_arrived(landed(core, 0), recv.at[0])
+    swaps[0].start()
+    receive(core, 0)
+    pair_sends(me, core, ref.out_c, ref.land_c, send.at[1], (recv.at[1],))
+    pair_arrived(landed(core, 1), recv.at[6])
+    swaps[1].start()
+    receive(core, 1)
+    for part in range(2):
+        pair_arrived(landed(1 - core, part), recv.at[2 + 5 * part])
+        receive(1 - core, part)
     mask = ref.bias[...]
 
     def pair(i, carry):
         @pl.when(i == 6)
         def _():
-            pair_arrived(core, ref.land_c, recv.at[1])
+            pair_arrived(ref.land_c.at[core], recv.at[1])
             swap_c.start()
 
         for u in range(2):
@@ -234,20 +256,21 @@
     lax.fori_loop(0, HEADS // 2, pair, 0)
 
     def upstream_arrived():
-        sibling_arrived(core, ref.land_c, recv.at[3])
+        pair_arrived(ref.land_c.at[1 - core], recv.at[3])
         for half in range(2):
             for part in range(2):
                 at = half * 512 + part * 256
                 pieces = ref.land_c[half, part * 32 : part * 32 + 32]
                 ref.upstream[at : at + 256, :] = unpack(pieces).astype(BF16)
+        ref.permuted[...] = dot(ref.upstream[...], ref.order_b[...], NN).astype(BF16)
 
     def finish():
-        swap_p.wait_send()
-        swap_c.wait_send()
+        for swap in (*swaps, swap_c):
+            swap.wait_send()
         pair_sent(core, ref.out_p, send.at[0])
         pair_sent(core, ref.out_c, send.at[1])
 
-    return upstream_arrived, finish
+    return slot, upstream_arrived, finish
 
 
 def backward_head(query, key, value, bias, attended, upstream, lse):
@@ -297,23 +320,28 @@
     return values * half, derivative
 
 
-CHUNK = 256
-
-
-def row_order():
+CHUNK = 512
+
+
+def row_order(to_yzx, sizes):
     place = lax.broadcasted_iota(jnp.int32, (D, D), 1)
-    y, z, x, j = place >> 7, (place >> 4) & 7, (place >> 2) & 3, place & 3
-    channel = (z << 6) + (x << 4) + (y << 2) + j
+    rest, parts = place >> 2, []
+    for size in reversed(sizes):
+        parts.insert(0, rest & (size - 1))
+        rest = rest >> (size.bit_length() - 1)
+    y, z, x = to_yzx(*parts)
+    channel = (z << 6) + (x << 4) + (y << 2) + (place & 3)
     return (lax.broadcasted_iota(jnp.int32, (D, D), 0) == channel).astype(BF16)
 
 
 def feed_forward(me, core, ref, upstream_arrived, part_a, part_b):
     sibling = (me, 1 - core)
     chunks = PATCH // CHUNK
+    half = chunks // 2
     proj, fc1, fc2 = ref.proj, ref.fc1, ref.fc2
 
     def place(i):
-        return lax.rem(i + 2 * (1 - core), chunks)
+        return lax.rem(i + half * (1 - core), chunks)
 
     def span(k):
         return pl.ds(pl.multiple_of(k * CHUNK, CHUNK), CHUNK)
@@ -360,17 +388,16 @@
         act_low = activation.astype(BF16)
         ref.act[at, :] = act_low
         partial = dot(act_low, fc2[...], NN).astype(BF16)
-        if i < 2:
+        if i < half:
             ref.snd2[i * CHUNK : (i + 1) * CHUNK, :] = partial
             copy2(i).start()
         else:
-            ref.own2[(i - 2) * CHUNK : (i - 1) * CHUNK, :] = partial
+            ref.own2[(i - half) * CHUNK : (i - half + 1) * CHUNK, :] = partial
         d_low = (dot(ref.upstream[at, :], fc2[...], NT) * derivative).astype(BF16)
         ref.d_pre[at, :] = d_low
         ref.snd3[at, :] = dot(d_low, fc1[...], NT).astype(BF16)
         copy3(k).start()
 
-    ref.permuted[...] = dot(ref.upstream[...], row_order(), NN).astype(BF16)
     for part in range(4):
         cols = slice(part * 256, part * 256 + 256)
         grad = dot(ref.permuted[...], ref.act[:, cols], TN).astype(BF16)
@@ -402,18 +429,18 @@
     ref.grad_a[:, :, :, FF:AW] = grad.reshape(NZ, NX, 16, AW - FF)
     part_a.start()
 
-    for i in range(2):
+    for i in range(half):
         copy2(i).wait_recv()
         own = slice(i * CHUNK, (i + 1) * CHUNK)
         added = ref.own2[own, :].astype(F32) + ref.rcv2[own, :].astype(F32)
-        total = ref.mixed[span(place(i + 2)), :] + added
-        ref.block[i * 32 : i * 32 + 32] = pack(total.astype(BF16).astype(F32))
+        total = ref.mixed[span(place(i + half)), :] + added
+        ref.block[i * CHUNK // 8 : (i + 1) * CHUNK // 8] = pack(total.astype(BF16).astype(F32))
 
     def finish():
         for k in range(chunks):
             copy1(k).wait_send()
             copy3(k).wait_send()
-        for i in range(2):
+        for i in range(half):
             copy2(i).wait_send()
 
     return finish
@@ -503,6 +530,87 @@
         for phase in range(3):
             for one in self.copies(phase):
                 one.wait_send()
+
+
+class PlaneReduceScatter:
+    def __init__(self, me, core, grad, scratch):
+        z, x, y = lax.div(me, NX * NY), lax.rem(lax.div(me, NY), NX), lax.rem(me, NY)
+        self.core, self.grad, self.place = core, grad, (z, x, y)
+        self.land_0, self.mid, self.land_1, self.send, self.recv = scratch
+        at = [(lax.rem(x + d // NY, NX), lax.rem(y + d % NY, NY)) for d in range(NX * NY)]
+        self.plane = [((z * NX + x2) * NY + y2, x2, y2) for x2, y2 in at]
+        other_z = [lax.rem(z + d, NZ) for d in range(NZ)]
+        self.line = [((z2 * NX + x) * NY + y, z2) for z2 in other_z]
+
+    def copy(self, k, src, dst, peer):
+        return pltpu.make_async_remote_copy(
+            src_ref=src,
+            dst_ref=dst,
+            send_sem=self.send.at[k],
+            recv_sem=self.recv.at[k],
+            device_id=(peer, self.core),
+            device_id_type=MESH,
+        )
+
+    def group(self, z):
+        return pl.ds(pl.multiple_of(lax.div(z, 4) * 16, 16), 16)
+
+    def copies(self, phase):
+        if phase == 0:
+            return [
+                self.copy(d - 1, self.grad.at[x, y], self.land_0.at[d - 1], peer)
+                for d, (peer, x, y) in enumerate(self.plane)
+                if d
+            ]
+        base = NX * NY - 2
+        return [
+            self.copy(base + d, self.mid.at[self.group(z), :], self.land_1.at[d - 1], peer)
+            for d, (peer, z) in enumerate(self.line)
+            if d
+        ]
+
+    def start(self):
+        for one in self.copies(0):
+            one.start()
+
+    def second(self):
+        for one in self.copies(0):
+            one.wait_recv()
+        _, x, y = self.place
+        total = self.grad[x, y].astype(F32)
+        for d in range(NX * NY - 1):
+            total = total + self.land_0[d].astype(F32)
+        self.mid[...] = total.astype(BF16)
+        for one in self.copies(1):
+            one.start()
+
+    def result(self):
+        for one in self.copies(1):
+            one.wait_recv()
+        z = self.place[0]
+        total = self.mid[self.group(z), :].astype(F32)
+        for d in range(NZ - 1):
+            total = total + self.land_1[d].astype(F32)
+        result = total[0:4]
+        for other in range(1, 4):
+            part = total[4 * other : 4 * other + 4]
+            result = jnp.where(lax.rem(z, 4) == other, part, result)
+        return result
+
+    def finish(self):
+        for phase in range(2):
+            for one in self.copies(phase):
+                one.wait_send()
+
+
+def plane_scratch(columns):
+    return [
+        pltpu.VMEM((NX * NY - 1, 32, columns), BF16),
+        pltpu.VMEM((32, columns), BF16),
+        pltpu.VMEM((NZ - 1, 16, columns), BF16),
+        pltpu.SemaphoreType.DMA((NX * NY + NZ - 2,)),
+        pltpu.SemaphoreType.DMA((NX * NY + NZ - 2,)),
+    ]
 
 
 def reduce_scratch(columns):
@@ -549,52 +657,65 @@
     grad_a=((NZ, NX, 16, AW), BF16),
     grad_b=((NY, NZ, 16, BW), BF16),
     grad_qa=((NZ, NX, 16, QA), BF16),
-    grad_qb=((NZ, NX, 16, QB), BF16),
+    grad_qb=((NX, NY, 32, QB), BF16),
+    land=((2, PAIRS, 16, D // 2), BF16),
+    weight=((3, D, 256), BF16),
+    proj=((256, D), BF16),
+    fc1=((D, FF), BF16),
+    fc2=((FF, D), BF16),
+    order_b=((D, D), BF16),
+    order_q=((D, D), BF16),
 )
-SEMAPHORES = dict(pair_send=(6,), pair_recv=(6,), core_send=(3, 4), core_recv=(3, 4))
-INPUTS = ("points", "cotangent", "patch", "weight", "proj", "fc1", "fc2")
-OUTPUTS = ("land", "slot_out", "sums_a", "sums_b", "sums_qa", "sums_qb")
+SEMAPHORES = dict(near=(4,), pair_send=(7,), pair_recv=(8,), core_send=(3, 4), core_recv=(3, 4))
+INPUTS = ("points", "cotangent", "patch", "far_weight", "far_proj", "far_fc1", "far_fc2")
+WEIGHTS = ("weight", "proj", "fc1", "fc2")
+OUTPUTS = ("rows_out", "sums_a", "sums_b", "sums_qa", "sums_qb")
 
 
 def block_kernel(*refs):
     names = (*INPUTS, *OUTPUTS, *SCRATCH, *SEMAPHORES)
     ref = types.SimpleNamespace(**dict(zip(names, refs)))
     rest = refs[len(names) :]
+    ref.loads = [
+        pltpu.make_async_copy(getattr(ref, "far_" + name), getattr(ref, name), ref.near.at[k])
+        for k, name in enumerate(WEIGHTS)
+    ]
     me, core = lax.axis_index("dp"), lax.axis_index("mp")
     parts = [
         ReduceScatter(me, core, first, grad, rest[7 * i : 7 * i + 7])
         for i, (first, grad) in enumerate(
-            ((True, ref.grad_a), (False, ref.grad_b), (True, ref.grad_qa), (True, ref.grad_qb))
+            ((True, ref.grad_a), (False, ref.grad_b), (True, ref.grad_qa))
         )
     ]
-    part_a, part_b, part_qa, part_qb = parts
-    others = [p for axis in part_a.peers for p in axis[1:]]
-    upstream_arrived, finish_attend = dispatch_and_attend(me, core, ref, others)
+    part_qb = PlaneReduceScatter(me, core, ref.grad_qb, rest[21:])
+    part_a, part_b, part_qa = parts
+    others = [peer for peer, *_ in (*part_qb.plane[1:], *part_qb.line[1:])]
+    slot, upstream_arrived, finish_attend = dispatch_and_attend(me, core, ref, others)
     finish_feed = feed_forward(me, core, ref, upstream_arrived, part_a, part_b)
     land, block, d_qkv = ref.land, ref.block, ref.d_qkv
     send, recv = ref.pair_send, ref.pair_recv
-    pair_sends(me, core, block, land, send.at[4], recv.at[4])
-    swap = to_sibling(me, core, land, send.at[5], recv.at[5])
+    pair_sends(me, core, block, land, send.at[4], (recv.at[4],), back=True)
+    swap = to_sibling(me, core, land.at[core], send.at[5], recv.at[5])
     finish_attend()
     mask = ref.bias[...]
 
-    def project(first, last, out):
+    def project(first, last):
         rows = (last - first) * HEAD_DIM
         heads = [d_qkv[j, first:last].reshape(rows, PATCH) for j in range(3)]
-        grad = dot(jnp.concatenate(heads, axis=0), ref.normed[...], NN)
-        out[...] = grad.T.astype(BF16).reshape(out.shape)
+        return dot(jnp.concatenate(heads, axis=0), ref.normed[...], NN)
 
     def pair(i, carry):
-        @pl.when(i == 5)
+        @pl.when(i == SECOND)
         def _():
             part_a.second()
             part_b.second()
 
         @pl.when(i == FIRST_HEADS // 2)
         def _():
-            project(0, FIRST_HEADS, ref.grad_qa)
+            grad = project(0, FIRST_HEADS).T.astype(BF16)
+            ref.grad_qa[...] = grad.reshape(NZ, NX, 16, QA)
             part_qa.start()
-            pair_arrived(core, land, recv.at[4])
+            pair_arrived(land.at[core], recv.at[4])
             swap.start()
 
         for u in range(2):
@@ -609,23 +730,30 @@
         return carry
 
     lax.fori_loop(0, HEADS // 2, pair, 0)
-    project(FIRST_HEADS, HEADS, ref.grad_qb)
+    grad = dot(project(FIRST_HEADS, HEADS).astype(BF16), ref.order_q[...], NN)
+    ref.grad_qb[...] = grad.T.astype(BF16).reshape(NX, NY, 32, QB)
     part_qb.start()
     part_a.third()
     part_b.third()
     part_qa.second()
     part_qb.second()
+    part_qa.third()
+    pair_arrived(land.at[1 - core], recv.at[5])
+    total = None
+    for half in range(2):
+        place = lax.broadcasted_iota(jnp.int32, (PATCH // 2, ROWS), 0) + half * (PATCH // 2)
+        chosen = (place == slot).astype(BF16)
+        part = dot(chosen, unpack(land[half]).astype(BF16), TN)
+        total = part if total is None else total + part
+    ref.rows_out[...] = total.astype(BF16)
     ref.sums_a[...] = part_a.result()
     ref.sums_b[...] = part_b.result()
-    part_qa.third()
-    part_qb.third()
-    sibling_arrived(core, land, recv.at[5])
     swap.wait_send()
     pair_sent(core, block, send.at[4])
     finish_feed()
     ref.sums_qa[...] = part_qa.result()
     ref.sums_qb[...] = part_qb.result()
-    for part in parts:
+    for part in (*parts, part_qb):
         part.finish()
 
 
@@ -633,14 +761,13 @@
     return pl.pallas_call(
         block_kernel,
         out_shape=(
-            jax.ShapeDtypeStruct((2, PAIRS, 16, D // 2), BF16),
-            jax.ShapeDtypeStruct((8, ROWS), jnp.int32),
+            jax.ShapeDtypeStruct((ROWS, D), BF16),
             jax.ShapeDtypeStruct((4, AW), F32),
             jax.ShapeDtypeStruct((4, BW), F32),
             jax.ShapeDtypeStruct((4, QA), F32),
             jax.ShapeDtypeStruct((4, QB), F32),
         ),
-        in_specs=[VMEM] * len(INPUTS),
+        in_specs=[VMEM] * 3 + [pl.BlockSpec(memory_space=pl.ANY)] * len(WEIGHTS),
         out_specs=(VMEM,) * len(OUTPUTS),
         scratch_shapes=[
             *(pltpu.VMEM(*shape) for shape in SCRATCH.values()),
@@ -648,7 +775,7 @@
             *reduce_scratch(AW),
             *reduce_scratch(BW),
             *reduce_scratch(QA),
-            *reduce_scratch(QB),
+            *plane_scratch(QB),
         ],
         compiler_params=params(collective_id=1, has_side_effects=True),
         name="block",
@@ -656,16 +783,9 @@
 
 
 def finish_kernel(
-    land, slot, sums_a, sums_b, sums_qa, sums_qb, rows_out, qkv_out, proj_out, fc1_out, fc2_out
+    rows, sums_a, sums_b, sums_qa, sums_qb, rows_out, qkv_out, proj_out, fc1_out, fc2_out
 ):
-    total = None
-    for half in range(2):
-        place = lax.broadcasted_iota(jnp.int32, (PATCH // 2, ROWS), 0) + half * (PATCH // 2)
-        chosen = (place == slot[0:1, :]).astype(BF16)
-        part = dot(chosen, unpack(land[half]).astype(BF16), TN)
-        total = part if total is None else total + part
-    rows_out[...] = total.astype(BF16)
-
+    rows_out[...] = rows[...]
     fc1_out[...] = sums_a[:, :FF]
     proj_out[...] = sums_a[:, FF:]
     fc2_out[...] = sums_b[...]
@@ -686,7 +806,7 @@
             jax.ShapeDtypeStruct((4, FF), F32),
             jax.ShapeDtypeStruct((4, FF), F32),
         ),
-        in_specs=[VMEM] * 6,
+        in_specs=[VMEM] * 5,
         out_specs=(VMEM,) * 5,
         compiler_params=params(),
         name="finish",

time: 128 us -> 122 us (0.953)
  Pallas kernels: 128 us -> 122 us
    pallas_call x1, Pallas kernels: 125 us -> 120 us  [whole_block(): pl.pallas_call(block_kernel, out_shape=(jax.ShapeDtypeStruct((ROWS, D), B...]
where the time goes in v4:
time: 122 us
  Pallas kernels  122 us (100%)
    pallas_call x1, Pallas kernels, whole_block(): pl.pallas_call(block_kernel, out_shape=(jax.ShapeDtypeStruct((ROWS, D), B...  120 us

profile of v4, /device:TPU:1, one launch (start us, length us, event | category | flops | bytes accessed | tf_op | source)
XLA Modules:
  0.0 122.2 jit_solution(3845914631415510871)
XLA Ops:
  0.6 119.7 %block.1 = (bf16[512,512]{1,0:T(8,128)(2,1)}, f32[4,1280]{1,0:T(4,128)}, f32[4,1024]{1,0:T(4,128)}, f32[4,576]{1,0:T(4,128)}, f32[4,192]{1,0:T(4,128)}) custom-call(bf16[512,512]{1,0:T(8,128)(2,1)} %refs_0_.1, bf16[512,512]{1,0:T(8,128)(2,1)} %refs_1_.1, s32[1,512]{1,0:T(1,128)} %bitcast.6, bf16[3,512,256]{2,1,0:T(8,128)(2,1)} %bitcast.5, ...), custom_call_target="tpu_custom_call" | custom-call | tf_op jit(solution)/shard_map/block/pallas_call | solution.py:761
  120.3 1.9 %finish.1 = (bf16[512,512]{1,0:T(8,128)(2,1)}, f32[3,4,256]{2,1,0:T(4,128)}, f32[4,256]{1,0:T(4,128)}, f32[4,1024]{1,0:T(4,128)}, f32[4,1024]{1,0:T(4,128)}) custom-call(bf16[512,512]{1,0:T(8,128)(2,1)} %get-tuple-element.15.rows, f32[4,1280]{1,0:T(4,128)} %get-tuple-element.16.sums_a, f32[4,1024]{1,0:T(4,128)} %get-tuple-element.17.sums_b, ...), custom_call_target="tpu_custom_call" | custom-call | tf_op jit(solution)/shard_map/finish/pallas_call | solution.py:800

commit v5 on v4

--- a/solution.py
+++ b/solution.py
@@ -187,6 +187,8 @@
     for load in ref.loads:
         load.start()
     pair_greet(me, core, others)
+    for load in ref.loads[:3]:
+        load.wait()
     slot = slot_rows(ref.patch[...], me)
     place = lax.broadcasted_iota(jnp.int32, (PATCH // 2, ROWS), 0) + core * (PATCH // 2)
     chosen = (place == slot).astype(BF16)
@@ -226,7 +228,7 @@
             projected = dot(ref.weight[j], normed, ((0,), (1,))).astype(BF16)
             ref.qkv[j, :, :, at] = projected.reshape(HEADS, HEAD_DIM, 256)
 
-    for load in ref.loads:
+    for load in ref.loads[3:]:
         load.wait()
     pair_arrived(landed(core, 0), recv.at[0])
     swaps[0].start()
@@ -241,19 +243,19 @@
     mask = ref.bias[...]
 
     def pair(i, carry):
-        @pl.when(i == 6)
+        @pl.when(i == 3)
         def _():
             pair_arrived(ref.land_c.at[core], recv.at[1])
             swap_c.start()
 
-        for u in range(2):
-            h = 2 * i + u
+        for u in range(4):
+            h = 4 * i + u
             result, lse = forward_head(ref.qkv[0, h], ref.qkv[1, h], ref.qkv[2, h], mask)
             ref.attended[h] = result
             ref.lse[h] = jnp.broadcast_to(lse, (8, PATCH))
         return carry
 
-    lax.fori_loop(0, HEADS // 2, pair, 0)
+    lax.fori_loop(0, HEADS // 4, pair, 0)
 
     def upstream_arrived():
         pair_arrived(ref.land_c.at[1 - core], recv.at[3])
@@ -659,6 +661,9 @@
     grad_qa=((NZ, NX, 16, QA), BF16),
     grad_qb=((NX, NY, 32, QB), BF16),
     land=((2, PAIRS, 16, D // 2), BF16),
+    patch=((1, ROWS), jnp.int32),
+    points=((ROWS, D), BF16),
+    cotangent=((ROWS, D), BF16),
     weight=((3, D, 256), BF16),
     proj=((256, D), BF16),
     fc1=((D, FF), BF16),
@@ -666,9 +671,9 @@
     order_b=((D, D), BF16),
     order_q=((D, D), BF16),
 )
-SEMAPHORES = dict(near=(4,), pair_send=(7,), pair_recv=(8,), core_send=(3, 4), core_recv=(3, 4))
-INPUTS = ("points", "cotangent", "patch", "far_weight", "far_proj", "far_fc1", "far_fc2")
-WEIGHTS = ("weight", "proj", "fc1", "fc2")
+SEMAPHORES = dict(near=(7,), pair_send=(7,), pair_recv=(8,), core_send=(3, 4), core_recv=(3, 4))
+LOADED = ("patch", "points", "cotangent", "weight", "proj", "fc1", "fc2")
+INPUTS = tuple("far_" + name for name in LOADED)
 OUTPUTS = ("rows_out", "sums_a", "sums_b", "sums_qa", "sums_qb")
 
 
@@ -678,7 +683,7 @@
     rest = refs[len(names) :]
     ref.loads = [
         pltpu.make_async_copy(getattr(ref, "far_" + name), getattr(ref, name), ref.near.at[k])
-        for k, name in enumerate(WEIGHTS)
+        for k, name in enumerate(LOADED)
     ]
     me, core = lax.axis_index("dp"), lax.axis_index("mp")
     parts = [
@@ -767,7 +772,7 @@
             jax.ShapeDtypeStruct((4, QA), F32),
             jax.ShapeDtypeStruct((4, QB), F32),
         ),
-        in_specs=[VMEM] * 3 + [pl.BlockSpec(memory_space=pl.ANY)] * len(WEIGHTS),
+        in_specs=[pl.BlockSpec(memory_space=pl.ANY)] * len(INPUTS),
         out_specs=(VMEM,) * len(OUTPUTS),
         scratch_shapes=[
             *(pltpu.VMEM(*shape) for shape in SCRATCH.values()),
@@ -815,9 +820,9 @@
 
 def per_device(points, patch_of, qkv_weight, proj_weight, fc1_weight, fc2_weight, cotangent):
     landed = whole_block(
+        patch_of.reshape(1, ROWS),
         points,
         cotangent,
-        patch_of.reshape(1, ROWS),
         qkv_weight.transpose(1, 0, 2),
         proj_weight,
         fc1_weight,

time: 122 us -> 121 us (level)
  Pallas kernels: 122 us -> 120 us
    pallas_call x1, Pallas kernels: 120 us -> 118 us  [whole_block(): pl.pallas_call(block_kernel, out_shape=(jax.ShapeDtypeStruct((ROWS, D), B...]
where the time goes in v5:
time: 121 us
  Pallas kernels  120 us (99%)
    pallas_call x1, Pallas kernels, whole_block(): pl.pallas_call(block_kernel, out_shape=(jax.ShapeDtypeStruct((ROWS, D), B...  118 us

profile of v5, /device:TPU:1, one launch (start us, length us, event | category | flops | bytes accessed | tf_op | source)
XLA Modules:
  0.0 120.8 jit_solution(17248436857850016203)
XLA Ops:
  0.6 118.2 %block.1 = (bf16[512,512]{1,0:T(8,128)(2,1)}, f32[4,1280]{1,0:T(4,128)}, f32[4,1024]{1,0:T(4,128)}, f32[4,576]{1,0:T(4,128)}, f32[4,192]{1,0:T(4,128)}) custom-call(s32[1,512]{1,0:T(1,128)} %bitcast.6, bf16[512,512]{1,0:T(8,128)(2,1)} %refs_1_.1, bf16[512,512]{1,0:T(8,128)(2,1)} %refs_2_.1, bf16[3,512,256]{2,1,0:T(8,128)(2,1)} %bitcast.5, ...), custom_call_target="tpu_custom_call" | custom-call | tf_op jit(solution)/shard_map/block/pallas_call | solution.py:766
  118.9 1.9 %finish.1 = (bf16[512,512]{1,0:T(8,128)(2,1)}, f32[3,4,256]{2,1,0:T(4,128)}, f32[4,256]{1,0:T(4,128)}, f32[4,1024]{1,0:T(4,128)}, f32[4,1024]{1,0:T(4,128)}) custom-call(bf16[512,512]{1,0:T(8,128)(2,1)} %get-tuple-element.15.rows, f32[4,1280]{1,0:T(4,128)} %get-tuple-element.16.sums_a, f32[4,1024]{1,0:T(4,128)} %get-tuple-element.17.sums_b, ...), custom_call_target="tpu_custom_call" | custom-call | tf_op jit(solution)/shard_map/finish/pallas_call | solution.py:805
